TPU v7x, 128 devices: a whole 4x4x4 slice. The times are simulated.
128 devices in a mesh: ctx: 8 (over y_lo, x), exp: 4 (over y_hi, core), fsdp: 4 (over z).
Axes of the slice: x: 4, y: 4 (y_hi: 2, y_lo: 2; y = y_hi * 2 + y_lo), z: 4, core: 2. Of those that a mesh axis runs over, the one named last changes fastest.
Arguments:
- inputs: bfloat16 [16, 1024, 1024], P(('exp', 'fsdp'), 'ctx'), may hold values from -6 to 6
- cotangent: bfloat16 [16, 1024, 1024], P(('exp', 'fsdp'), 'ctx'), may hold values from -6 to 6
- w_query: bfloat16 [1024, 1024], P(('ctx', 'exp', 'fsdp')), may hold values from -0.1875 to 0.1875
- key_weight: bfloat16 [1024, 512], P(('ctx', 'exp', 'fsdp')), may hold values from -0.1875 to 0.1875
- value_weight: bfloat16 [1024, 512], P(('ctx', 'exp', 'fsdp')), may hold values from -0.1875 to 0.1875
- w_output: bfloat16 [1024, 1024], P(None, ('ctx', 'exp', 'fsdp')), may hold values from -1.5 to 1.5
- w_router: bfloat16 [1024, 32], P(('ctx', 'exp', 'fsdp')), may hold values from -0.09375 to 0.09375
- norm_gains: bfloat16 [2176], P(('ctx', 'exp', 'fsdp')), may hold values from 0.5 to 1.5
- w_gate_up: bfloat16 [32, 1024, 1024], P('exp', ('ctx', 'fsdp')), may hold values from -0.1875 to 0.1875
- w_down: bfloat16 [32, 512, 1024], P('exp', None, ('ctx', 'fsdp')), may hold values from -1 to 1
- seq_lengths: int32 [16, 4], P(('exp', 'fsdp')), may hold values from 1 to 897, 1024 in all within a row
- block_map: int32 [16, 8], P(('exp', 'fsdp')), may hold values from 0 to 7, each once within a row
- routes: int32 [16, 1024, 8], P(('exp', 'fsdp'), 'ctx'), may hold values from 0 to 31, all different within a row; in each aligned block of 128 rows (0 to 127, 128 to 255, ..., all dimensions but the last counted through in order) at most 80 rows name the same one
- priority: int32 [16, 8, 128], P(('exp', 'fsdp'), 'ctx'), may hold values from 0 to 127, each once within a row
Outputs:
- output: bfloat16 [16, 1024, 1024], P(('exp', 'fsdp'), 'ctx')
- grad_inputs: bfloat16 [16, 1024, 1024], P(('exp', 'fsdp'), 'ctx')
- grad_query: float32 [1024, 1024], P(('ctx', 'exp', 'fsdp'))
- grad_key: float32 [1024, 512], P(('ctx', 'exp', 'fsdp'))
- grad_value: float32 [1024, 512], P(('ctx', 'exp', 'fsdp'))
- grad_w_output: float32 [1024, 1024], P(None, ('ctx', 'exp', 'fsdp'))
- grad_router: float32 [1024, 32], P(('ctx', 'exp', 'fsdp'))
- grad_gains: float32 [2176], P(('ctx', 'exp', 'fsdp'))
- grad_gate_up: float32 [32, 1024, 1024], P('exp', ('ctx', 'fsdp'))
- grad_down: float32 [32, 512, 1024], P('exp', None, ('ctx', 'fsdp'))
Inputs may be any that keep to these rules, and one draw needn't show every extreme that they name: `seq_lengths`: the 4 lengths of a group add up to 1024; the longest has exactly 897 tokens. `block_map`: each row is a permutation of the 8 blocks. `routes`: each slot names 8 different experts; among the slots of one place no expert is named more than 2 * 40 times, and some expert exactly that often. `priority`: each place's row is a permutation.
All inputs are finite; a program needn't handle non-finite values.
Results may differ from a plain program's by a relative error of at most 0.03.
Values may be sent and summed in bfloat16 or wider, within the bound.
A program may use at most 192 MiB of HBM per device.

v0:
```python
import math
import types

import jax
import jax.numpy as jnp
from jax import lax
from jax.experimental import pallas as pl
from jax.experimental.pallas import tpu as pltpu
from jax.sharding import Mesh
from jax.sharding import PartitionSpec as P

HEADS = 16
KV_HEADS = 8
DIM = 1024
HEAD = 64
FF = 512
EXPERTS = 32
TOPK = 8
ROWS = 128
GTOK = 1024
CAP = 40
GAINS = 17
WIDE = 3 * FF
PART = 8 * CAP
BF = jnp.bfloat16
F32 = jnp.float32
I32 = jnp.int32

ALL = ("yl", "x", "yh", "co", "z")
SIZES = (2, 4, 2, 2, 4)
SPAN = dict(zip(ALL, SIZES))
CTX = ("yl", "x")
EP = ("yh", "co", "yl", "z")
WT = ("yl", "x", "z")
LONG = ("yl", "x", "yh")


def linear(axes):
    index = 0
    for axis in axes:
        index = index * SPAN[axis] + lax.axis_index(axis)
    return index


def device(axes, index):
    at = {}
    for axis in reversed(axes):
        at[axis] = lax.rem(index, SPAN[axis])
        index = index // SPAN[axis]
    return tuple(at[axis] if axis in at else lax.axis_index(axis) for axis in ALL)


def flip(a, b, bits):
    return sum(lax.rem(a // 2**n + b // 2**n, 2) * 2**n for n in range(bits))


def greet(axes):
    n = math.prod(SPAN[axis] for axis in axes)
    me = linear(axes)
    barrier = pltpu.get_barrier_semaphore()

    def signal(i, carry):
        pl.semaphore_signal(
            barrier,
            inc=1,
            device_id=device(axes, lax.rem(me + i, n)),
            device_id_type=pl.DeviceIdType.MESH,
        )
        return carry

    lax.fori_loop(1, n, signal, 0)
    pl.semaphore_wait(barrier, n - 1)


class Send:
    def __init__(self, axes, part, slot, sems):
        self.axes, self.part, self.slot, self.sems = axes, part, slot, sems
        self.n = math.prod(SPAN[axis] for axis in axes)
        self.bits = self.n.bit_length() - 1
        self.me = linear(axes)

    def partner(self, i):
        return flip(self.me, i, self.bits)

    def copy(self, i):
        to = self.partner(i)
        return pltpu.make_async_remote_copy(
            src_ref=self.part(to),
            dst_ref=self.slot(self.me),
            send_sem=self.sems.at[0, i],
            recv_sem=self.sems.at[1, i],
            device_id=device(self.axes, to),
            device_id_type=pl.DeviceIdType.MESH,
        )

    def own(self):
        return pltpu.make_async_copy(self.part(self.me), self.slot(self.me), self.sems.at[0, 0])

    def each(self, act, low=1, high=None):
        def one(i, carry):
            act(self.copy(i))
            return carry

        lax.fori_loop(low, self.n if high is None else high, one, 0)

    def start(self, own=True):
        if own:
            self.own().start()
        self.each(lambda copy: copy.start())

    def arrived(self, low=1, high=None):
        self.each(lambda copy: copy.wait_recv(), low, high)

    def sent(self):
        self.each(lambda copy: copy.wait_send())

    def wait(self, own=True):
        if own:
            self.own().wait()
        self.each(lambda copy: copy.wait())


def dot(left, right, dims=((1,), (0,))):
    return lax.dot_general(left, right, (dims, ((), ())), preferred_element_type=F32)


def rms(v):
    return lax.rsqrt(jnp.mean(v * v, axis=-1, keepdims=True) + 1e-06)


def norm_back(v, scale, gain, upstream):
    weighted = upstream * gain
    inner = jnp.mean(weighted * v, axis=-1, keepdims=True)
    return scale * weighted - v * (scale * scale * scale) * inner, upstream * v * scale


def halves():
    lane = lax.broadcasted_iota(I32, (1, 128), 1)
    return lane < HEAD, lax.rem(lane, HEAD) < HEAD // 2


def head_mean(v, first):
    low = jnp.sum(jnp.where(first, v, 0.0), axis=1, keepdims=True)
    high = jnp.sum(jnp.where(first, 0.0, v), axis=1, keepdims=True)
    return jnp.where(first, low, high) * (1.0 / HEAD)


def head_rms(v, first):
    return lax.rsqrt(head_mean(v * v, first) + 1e-06)


def head_norm_back(v, gain, upstream, first):
    scale = head_rms(v, first)
    weighted = upstream * gain
    inner = head_mean(weighted * v, first)
    terms = jnp.sum(upstream * v * scale, axis=0, keepdims=True)
    return scale * weighted - v * (scale * scale * scale) * inner, terms


def turn_pair(v, cos, sin, front):
    return v * cos + jnp.where(front, -pltpu.roll(v, 96, 1), pltpu.roll(v, 32, 1)) * sin


def starts(tokens, ends):
    first = jnp.zeros_like(tokens)
    for end in ends:
        first = jnp.maximum(first, jnp.where(tokens >= end, end, 0))
    return first


def sequence_ends(lengths):
    ends, total = [], 0
    for i in range(3):
        total = total + lengths[i]
        ends.append(total)
    return ends


def gain_places():
    column = lax.broadcasted_iota(I32, (128, 128 * GAINS), 1)
    row = lax.broadcasted_iota(I32, (128, 128 * GAINS), 0)
    owner = (column * 3856) >> 16
    return row == owner, row == EXPERTS + column - owner * GAINS


def spread_gains(packed):
    owner, lane = gain_places()
    rows = dot(packed, owner.astype(F32).astype(BF), ((0,), (0,)))
    return jnp.sum(jnp.where(lane, rows, 0.0), axis=0, keepdims=True)


def pack_gains(row):
    owner, lane = gain_places()
    return dot(
        owner.astype(F32).astype(BF), jnp.where(lane, row, 0.0).astype(BF), ((1,), (1,))
    )


def merge(v):
    shape = v.shape
    return v.astype(F32).reshape(math.prod(shape[:-1]), shape[-1]).astype(BF)


def rows_of(j):
    return pl.ds(j * ROWS if isinstance(j, int) else pl.multiple_of(j * ROWS, ROWS), ROWS)


def layer_kernel(r):
    greet(ALL)
    place, seat_me = linear(CTX), linear(EP)
    spot, core, deep = lax.axis_index("x"), lax.axis_index("co"), lax.axis_index("z")
    first, front = halves()

    def bring(source, target):
        copy = pltpu.make_async_copy(source, target, r.s_stage.at[0, 0])
        copy.start()
        return copy

    send_picks = Send(CTX, lambda p: r.picks, lambda q: r.picks_to.at[q], r.s_picks)
    send_x = Send(CTX, lambda p: r.x, lambda q: r.x_to.at[q], r.s_x)
    send_heads = Send(
        ("yl", "x", "yh", "z"),
        lambda p: r.heads.at[p // 8],
        lambda q: r.heads_to.at[q // 4, core, lax.rem(q, 4)],
        r.s_heads,
    )
    swap_heads = Send(
        ("co",), lambda p: r.heads_to.at[:, core], lambda q: r.heads_to.at[:, q], r.s_heads_co
    )
    send_dz = Send(EP, lambda p: r.slots.at[p], lambda q: r.dz_to.at[q], r.s_dz)
    send_wide = Send(
        ("yl", "z"),
        lambda p: r.wide.at[p],
        lambda q: r.wide_to.at[q // 4, spot, lax.rem(q, 4)],
        r.s_wide,
    )
    pass_wide = Send(
        ("x",), lambda p: r.wide_to.at[:, spot], lambda q: r.wide_to.at[:, q], r.s_wide_x
    )
    send_out = Send(LONG, lambda p: r.out, lambda q: r.out_to.at[q, core, deep], r.s_out)
    pass_out = Send(
        ("z",), lambda p: r.out_to.at[:, core, deep], lambda q: r.out_to.at[:, core, q], r.s_out_z
    )
    swap_out = Send(
        ("co",), lambda p: r.out_to.at[:, core], lambda q: r.out_to.at[:, q], r.s_out_co
    )
    send_o = Send(CTX, lambda p: r.o_rows.at[p], lambda q: r.o_to.at[q], r.s_o)
    send_a2 = Send(EP, lambda p: r.slots.at[p], lambda q: r.a2_to.at[q], r.s_a2)
    send_gate = Send(EP, lambda p: r.gates.at[p], lambda q: r.gates_to.at[q], r.s_gate)
    send_y = Send(EP, lambda p: r.y_rows.at[p], lambda q: r.y_to.at[q], r.s_y)
    send_da = Send(EP, lambda p: r.da_rows.at[p], lambda q: r.da_to.at[q], r.s_da)
    send_grad = Send(("x",), lambda p: r.grad.at[:, p], lambda q: r.grad_to.at[:, q], r.s_grad)
    last_grad = Send(
        ("yl", "z"), lambda p: r.grad_mid.at[p], lambda q: r.grad_last.at[q], r.s_grad_last
    )
    send_do = Send(CTX, lambda p: r.do_rows.at[p], lambda q: r.do_to.at[q], r.s_do)
    send_da1 = Send(CTX, lambda p: r.x_to.at[p], lambda q: r.a_rows.at[rows_of(q)], r.s_da1)

    send_picks.start()
    send_x.start()
    send_wide.start()
    send_heads.start()
    send_out.start()

    send_picks.wait()
    mine = jnp.zeros((16, 128), I32)
    for p in range(8):
        mine = mine + r.picks_to[p] * (r.blocks[p] == place).astype(I32)
    expert = lax.broadcasted_iota(I32, (EXPERTS, ROWS), 0)
    named = jnp.zeros((EXPERTS, ROWS), jnp.bool_)
    for k in range(TOPK):
        named = named | (mine[k : k + 1] == expert)
    order = jnp.broadcast_to(mine[TOPK : TOPK + 1].astype(F32), (128, ROWS))
    before = (order.T < order).astype(F32).astype(BF)
    rank = jnp.where(named, dot(named.astype(F32).astype(BF), before), -1.0)
    seat = lax.broadcasted_iota(I32, (CAP, ROWS), 0).astype(F32)
    for e in range(EXPERTS):
        r.hot[pl.ds(e * CAP, CAP)] = (rank[e : e + 1] == seat).astype(F32)

    def fill(source):
        def one(i, carry):
            rows = r.hot[pl.ds(pl.multiple_of(i * 160, 160), 160)].astype(BF)
            r.slots[pl.ds(i * 4, 4)] = dot(rows, source[...]).reshape(4, CAP, DIM).astype(BF)
            return carry

        lax.fori_loop(0, 8, one, 0)

    fill(r.dz)
    send_dz.start()
    send_wide.wait()
    pass_wide.start(own=False)
    send_heads.wait()
    swap_heads.start(own=False)
    send_out.wait()
    pass_out.start(own=False)
    swap_heads.wait(own=False)

    packed = r.heads_to[...].astype(F32).reshape(128, 8, 384)
    r.w_heads[...] = packed[:, :, :256].reshape(DIM, 256).astype(BF)
    r.router[...] = packed[:, :, 256:].reshape(DIM, 128).astype(BF)
    gains = spread_gains(packed[:, 0, 256:].astype(BF))
    gain_one, gain_two, pair = gains[:, :DIM], gains[:, DIM : 2 * DIM], gains[:, 2 * DIM :]
    swapped = pltpu.roll(pair, HEAD, 1)
    gain_q, gain_k = jnp.where(first, pair, swapped), jnp.where(first, swapped, pair)
    ends = sequence_ends(r.lengths)
    lane = lax.broadcasted_iota(I32, (1, 128), 1)
    frequency = jnp.exp(
        lax.rem(lane, HEAD // 2).astype(F32) * (-2.0 * math.log(10000.0) / HEAD)
    )

    def project(j):
        at = rows_of(j)
        v = r.x_to[j].astype(F32)
        low = (v * rms(v) * gain_one).astype(BF)
        r.a_all[at] = low
        qkv = dot(low, r.w_heads[...])
        r.pre[at] = qkv
        token = j * ROWS + lax.broadcasted_iota(I32, (ROWS, 1), 0)
        angle = (token - starts(token, ends)).astype(F32) * frequency
        cos, sin = jnp.cos(angle), jnp.sin(angle)
        r.cos[at] = cos
        r.sin[at] = sin
        q, kv = qkv[:, :128], qkv[:, 128:]
        other = pltpu.roll(kv, HEAD, 1)
        k, val = jnp.where(first, kv, other), jnp.where(first, other, kv)
        r.qr[at] = turn_pair(q * head_rms(q, first) * gain_q, cos, sin, front).astype(BF)
        r.kr[at] = turn_pair(k * head_rms(k, first) * gain_k, cos, sin, front).astype(BF)
        r.vv[at] = val.astype(BF)

    send_x.own().wait()
    project(place)

    def arrive(i, carry):
        send_x.copy(i).wait()
        project(send_x.partner(i))
        return carry

    lax.fori_loop(1, 8, arrive, 0)

    def stacked(v):
        v = v.astype(F32)
        return jnp.concatenate(
            [jnp.where(first, v, 0.0), jnp.where(first, 0.0, v)], axis=0
        ).astype(BF)

    def beside(v):
        return jnp.where(first, v[:ROWS], v[ROWS:])

    def masked_scores(tile, q, width):
        scores = dot(q, r.kr[pl.ds(0, width)], ((1,), (1,))) * HEAD**-0.5
        token = tile * ROWS + lax.rem(lax.broadcasted_iota(I32, (2 * ROWS, 1), 0), ROWS)
        key = lax.broadcasted_iota(I32, (2 * ROWS, width), 1)
        return jnp.where((key <= token) & (key >= starts(token, ends)), scores, -1e30)

    for tile in range(8):
        width, at = ROWS * (tile + 1), rows_of(tile)
        scores = masked_scores(tile, stacked(r.qr[at]), width)
        top = jnp.max(scores, axis=1, keepdims=True)
        weight = jnp.exp(scores - top)
        total = jnp.sum(weight, axis=1, keepdims=True)
        result = beside(dot((weight * (1.0 / total)).astype(BF), r.vv[pl.ds(0, width)]))
        r.mixed[at] = result
        r.o_rows[tile] = result.astype(BF)
        r.level[at] = beside(jnp.broadcast_to(top + jnp.log(total), (2 * ROWS, 128)))
    send_o.start()
    pass_out.wait(own=False)
    swap_out.start(own=False)
    send_dz.wait()
    swap_out.wait(own=False)

    def lay(i, carry):
        r.w_out[rows_of(i)] = merge(r.out_to[pl.ds(2 * i, 2)])
        return carry

    lax.fori_loop(0, 8, lay, 0)

    send_o.wait()
    for h in range(8):
        r.ob[:, h * 128 : (h + 1) * 128] = r.o_to[h]
    x_own = r.x[...].astype(F32)
    dz = r.dz[...].astype(F32)
    x1 = x_own + dot(r.ob[...], r.w_out[...], ((1,), (1,)))
    r.x1[...] = x1
    r2 = rms(x1)
    r.a2[...] = (x1 * r2 * gain_two).astype(BF)
    logits = dot(r.router[...], r.a2[...], ((0,), (1,)))[:EXPERTS]
    weight = jnp.exp(logits - jnp.max(logits, axis=0, keepdims=True))
    probs = weight / jnp.sum(weight, axis=0, keepdims=True)
    chosen = jnp.where(named, probs, 0.0)
    total = jnp.sum(chosen, axis=0, keepdims=True)
    gate = chosen / total
    r.gate[...] = gate
    r.gates[:, 0, :] = gate
    r.gates[:, 1, :] = rank
    fill(r.a2)
    send_gate.start()
    send_a2.start()
    pass_wide.wait(own=False)
    send_gate.wait()
    send_a2.own().wait()

    w_all = r.wide_to.reshape(DIM, WIDE)
    w_gu, w_dn = w_all.at[:, : 2 * FF], w_all.at[:, 2 * FF :]

    def part_of(c):
        return flip(seat_me // 8, c, 2)

    def work(c, carry):
        send_a2.arrived(8 * c + (c == 0).astype(I32), 8 * c + 8)
        k8 = part_of(c) * 8
        at = pl.ds(pl.multiple_of(c * PART, PART), PART)
        a = merge(r.a2_to[pl.ds(k8, 8)])
        r.a_rows[at] = a
        staged = bring(r.dz_to.at[pl.ds(k8, 8)], r.stage)
        gu = dot(a, w_gu[...])
        g, up = gu[:, :FF], gu[:, FF:]
        s = 1.0 / (1.0 + jnp.exp(-g))
        hid = (g * s * up).astype(BF)
        r.hid[at] = hid
        y = dot(hid, w_dn[...], ((1,), (1,)))
        r.y_rows[pl.ds(k8, 8)] = y.reshape(8, CAP, DIM).astype(BF)

        @pl.when(c == 0)
        def _():
            send_y.own().start()

        send_y.each(lambda copy: copy.start(), 8 * c + (c == 0).astype(I32), 8 * c + 8)
        note = r.gates_to[pl.ds(k8, 8)]
        column = jnp.sum(
            jnp.where(note[:, 1:2] == seat[None], note[:, 0:1], 0.0), axis=2, keepdims=True
        )
        staged.wait()
        dy = r.stage[...].astype(F32) * column
        dy = dy.reshape(PART, DIM).astype(BF)
        r.dy[at] = dy
        dhid = dot(dy, w_dn[...])
        dgu = jnp.concatenate([dhid * up * s * (1.0 + g * (1.0 - s)), dhid * g * s], axis=1)
        dgu = dgu.astype(BF)
        r.dgu[at] = dgu
        da = dot(dgu, w_gu[...], ((1,), (1,)))
        r.da_rows[pl.ds(k8, 8)] = da.reshape(8, CAP, DIM).astype(BF)

        @pl.when(c == 0)
        def _():
            send_da.own().start()

        send_da.each(lambda copy: copy.start(), 8 * c + (c == 0).astype(I32), 8 * c + 8)
        return carry

    lax.fori_loop(0, 4, work, 0)
    send_a2.sent()

    def weigh(i, carry):
        to = send_grad.partner(i)
        for yl in range(2):
            at = pl.ds(pl.multiple_of((yl * 4 + to) * ROWS, ROWS), ROWS)
            gu = dot(r.a_rows[:, at], r.dgu[...], ((0,), (0,)))
            r.grad[yl, to, :, :, : 2 * FF] = gu.astype(BF).reshape(4, 32, 2 * FF)
            dn = dot(r.dy[:, at], r.hid[...], ((0,), (0,)))
            r.grad[yl, to, :, :, 2 * FF :] = dn.astype(BF).reshape(4, 32, FF)

        @pl.when(i < 4)
        def _():
            send_grad.copy(i).start()

        return carry

    lax.fori_loop(1, 5, weigh, 0)
    send_grad.own().start()

    send_y.own().wait()
    r.sum[...] = jnp.zeros_like(r.sum)

    def mix(c, carry):
        send_y.arrived(8 * c + (c == 0).astype(I32), 8 * c + 8)
        k8 = pl.multiple_of(part_of(c) * 8, 8)
        bring(r.y_to.at[pl.ds(k8, 8)], r.stage).wait()
        y = merge(r.stage[...])
        hot = r.hot[pl.ds(pl.multiple_of(k8 * CAP, PART), PART)]
        weights = (hot.reshape(8, CAP, ROWS) * r.gate[pl.ds(k8, 8)][:, None]).reshape(PART, ROWS)
        high = weights.astype(BF)
        low = (weights - high.astype(F32)).astype(BF)
        r.sum[...] += dot(high, y, ((0,), (0,))) + dot(low, y, ((0,), (0,)))
        pairs = dot(y, r.dz[...], ((1,), (1,))) * hot
        r.dgate[pl.ds(k8, 8)] = jnp.sum(pairs.reshape(8, CAP, ROWS), axis=1)
        return carry

    lax.fori_loop(0, 4, mix, 0)
    r.output[...] = (r.x1[...] + r.sum[...]).astype(BF)
    dgate = r.dgate[...]
    dc = jnp.where(named, dgate - jnp.sum(gate * dgate, axis=0, keepdims=True), 0.0) / total
    dl = probs * (dc - jnp.sum(probs * dc, axis=0, keepdims=True))
    dl = jnp.concatenate([dl, jnp.zeros((128 - EXPERTS, ROWS), F32)], axis=0).astype(BF)
    r.dl[...] = dl
    r.sum[...] = dot(dl, r.router[...], ((0,), (1,)))
    send_da.own().wait()

    def unmix(c, carry):
        send_da.arrived(8 * c + (c == 0).astype(I32), 8 * c + 8)
        k8 = pl.multiple_of(part_of(c) * 8, 8)
        hot = r.hot[pl.ds(pl.multiple_of(k8 * CAP, PART), PART)].astype(BF)
        bring(r.da_to.at[pl.ds(k8, 8)], r.stage).wait()
        r.sum[...] += dot(hot, merge(r.stage[...]), ((0,), (0,)))
        return carry

    lax.fori_loop(0, 4, unmix, 0)
    dx_two, terms_two = norm_back(r.x1[...], rms(r.x1[...]), gain_two, r.sum[...])
    gain_two_grad = jnp.sum(terms_two, axis=0, keepdims=True)
    r.dx1[...] = dz + dx_two
    r.db[...] = r.dx1[...].astype(BF)
    do = dot(r.db[...], r.w_out[...]).astype(BF)
    for h in range(8):
        r.do_rows[h] = do[:, h * 128 : (h + 1) * 128]
    send_do.start()

    swap_gwo = Send(("co",), lambda p: r.out_to.at[:, p], lambda q: r.gwo_co, r.s_gwo_co)
    pass_gwo = Send(("z",), lambda p: r.gwo_mid.at[:, p], lambda q: r.gwo_z.at[:, q], r.s_gwo_z)
    last_gwo = Send(LONG, lambda p: r.gwo_sum.at[p], lambda q: r.gwo_last.at[q], r.s_gwo)

    def spread_out(i, carry):
        part = dot(r.db[:, rows_of(i)], r.ob[...], ((0,), (0,)))
        r.out_to[pl.ds(2 * i, 2)] = part.reshape(2, 2, 4, 8, DIM).astype(BF)
        return carry

    lax.fori_loop(0, 8, spread_out, 0)
    swap_gwo.start(own=False)

    def add_core(i, carry):
        both = r.out_to[i, core].astype(F32) + r.gwo_mid[i].astype(F32)
        r.gwo_mid[i] = both.astype(BF)
        return carry

    send_do.wait()
    r.dk[...] = jnp.zeros_like(r.dk)
    r.dv[...] = jnp.zeros_like(r.dv)
    for tile in range(8):
        width, at = ROWS * (tile + 1), rows_of(tile)
        keys = pl.ds(0, width)
        q = stacked(r.qr[at])
        level = r.level[at]
        level = jnp.concatenate([level[:, :1], level[:, HEAD : HEAD + 1]], axis=0)
        probs_at = jnp.exp(masked_scores(tile, q, width) - level)
        do = r.do_to[tile]
        inner = head_mean(do.astype(F32) * r.mixed[at], first) * HEAD
        inner = jnp.concatenate([inner[:, :1], inner[:, HEAD : HEAD + 1]], axis=0)
        do = stacked(do)
        dp = dot(do, r.vv[keys], ((1,), (1,)))
        ds = (probs_at * (dp - inner)).astype(BF)
        r.dq[at] = beside(dot(ds, r.kr[keys])) * HEAD**-0.5
        r.dk[keys] += dot(ds, q, ((0,), (0,)))
        r.dv[keys] += dot(probs_at.astype(BF), do, ((0,), (0,)))

    swap_gwo.wait(own=False)
    bring(r.gwo_co, r.gwo_mid).wait()
    lax.fori_loop(0, 16, add_core, 0)
    pass_gwo.start()
    r.gain_one_grad[...] = jnp.zeros_like(r.gain_one_grad)
    r.gain_q_grad[...] = jnp.zeros_like(r.gain_q_grad)
    r.gain_k_grad[...] = jnp.zeros_like(r.gain_k_grad)

    def back(i, carry):
        j = send_da1.partner(lax.rem(i, 8))
        at = rows_of(j)
        cos, sin = r.cos[at], -r.sin[at]
        qkv = r.pre[at]
        q, kv = qkv[:, :128], qkv[:, 128:]
        k = jnp.where(first, kv, pltpu.roll(kv, HEAD, 1))
        dk, dv = r.dk[at] * HEAD**-0.5, r.dv[at]
        dk, dv = dk + pltpu.roll(dk, HEAD, 1), dv + pltpu.roll(dv, HEAD, 1)
        dq, terms = head_norm_back(q, gain_q, turn_pair(r.dq[at], cos, sin, front), first)
        r.gain_q_grad[...] += terms
        dk, terms = head_norm_back(k, gain_k, turn_pair(dk, cos, sin, front), first)
        r.gain_k_grad[...] += terms
        dqkv = jnp.concatenate([dq, jnp.where(first, dk, dv)], axis=1).astype(BF)
        r.dqkv[at] = dqkv
        da1 = dot(dqkv, r.w_heads[...], ((1,), (1,)))
        v = r.x_to[j].astype(F32)
        r.gain_one_grad[...] += jnp.sum(da1 * (v * rms(v)), axis=0, keepdims=True)
        r.x_to[j] = da1.astype(BF)

        @pl.when(i < 8)
        def _():
            send_da1.copy(i).start()

        return carry

    lax.fori_loop(1, 9, back, 0)
    send_da1.own().start()

    pair = jnp.where(
        first,
        r.gain_q_grad[...] + pltpu.roll(r.gain_q_grad[...], HEAD, 1),
        r.gain_k_grad[...],
    )
    gain_grads = pack_gains(
        jnp.concatenate([r.gain_one_grad[...], gain_two_grad, pair], axis=1)
    )
    r.side[...] = jnp.where(
        lax.broadcasted_iota(I32, (128, 8, 128), 1) == 0, gain_grads[:, None], 0.0
    ).reshape(DIM, 128) + dot(r.a2[...], r.dl[...], ((0,), (1,)))

    def small(i, carry):
        at = rows_of(i)
        part = dot(r.a_all[:, at], r.dqkv[...], ((0,), (0,)))
        part = jnp.concatenate([part, r.side[at]], axis=1)
        r.heads_to[pl.ds(2 * i, 2)] = part.reshape(2, 2, 4, 8, 384).astype(BF)
        return carry

    lax.fori_loop(0, 8, small, 0)
    swap_hg = Send(("co",), lambda p: r.heads_to.at[:, p], lambda q: r.hg_co, r.s_hg_co)
    pass_hg = Send(("z",), lambda p: r.hg_mid.at[:, p], lambda q: r.hg_z.at[q], r.s_hg_z)
    last_hg = Send(LONG, lambda p: r.hg_sum.at[p], lambda q: r.hg_last.at[q], r.s_hg)
    swap_hg.start(own=False)

    pass_gwo.wait()
    bring(r.gwo_z, r.out_to.at[:, 0]).wait()

    def add_deep(i, carry):
        total = sum(r.out_to[i, 0, n].astype(F32) for n in range(4))
        r.gwo_sum[i] = total.astype(BF)
        return carry

    lax.fori_loop(0, 16, add_deep, 0)
    last_gwo.start()
    send_grad.wait()
    bring(r.grad_to, r.wide_to).wait()

    def add_grad(i, carry):
        total = sum(
            r.wide_to[i // 4, n, lax.rem(i, 4)].astype(F32) for n in range(4)
        )
        r.grad_mid[i] = total.astype(BF)
        return carry

    lax.fori_loop(0, 8, add_grad, 0)
    last_grad.start()
    swap_hg.wait(own=False)
    r.hg_mid[...] = (r.heads_to[:, core].astype(F32) + r.hg_co[...].astype(F32)).astype(BF)
    pass_hg.start()
    pass_hg.wait()
    r.hg_sum[...] = sum(r.hg_z[n].astype(F32) for n in range(4)).astype(BF)
    last_hg.start()

    send_da1.wait()
    da1 = sum(r.a_rows[rows_of(n)].astype(F32) for n in range(8))
    x_own = r.x[...].astype(F32)
    dx_one, _ = norm_back(x_own, rms(x_own), gain_one, da1)
    r.grad_inputs[...] = (r.dx1[...] + dx_one).astype(BF)
    last_gwo.wait()
    r.grad_out[...] = sum(r.gwo_last[n].astype(F32) for n in range(16))
    last_grad.wait()
    last_hg.wait()
    r.head_grad[...] = sum(
        r.hg_last[...].astype(F32).reshape(8, 2, 8, 384)[:, n] for n in range(2)
    )
    send_y.sent()
    send_da.sent()


INPUTS = (
    ("lengths", pltpu.SMEM),
    ("blocks", pltpu.SMEM),
    ("x", pltpu.VMEM),
    ("heads", pltpu.VMEM),
    ("picks", pltpu.VMEM),
    ("dz", pltpu.VMEM),
    ("wide", pl.ANY),
    ("out", pltpu.VMEM),
)
OUTPUTS = (
    ("output", (ROWS, DIM), BF),
    ("grad_inputs", (ROWS, DIM), BF),
    ("head_grad", (8, 8, 384), F32),
    ("grad_out", (8, DIM), F32),
)
ROW_SLOTS = (EXPERTS, CAP, DIM)
LANDING = (
    ("grad_last", (8, 32, WIDE), BF),
    ("dz_to", ROW_SLOTS, BF),
    ("y_to", ROW_SLOTS, BF),
    ("da_to", ROW_SLOTS, BF),
    ("grad_to", (2, 4, 4, 32, WIDE), BF),
    ("gwo_co", (16, 4, 8, DIM), BF),
    ("gwo_z", (16, 4, 8, DIM), BF),
)
SCRATCH = (
    ("picks_to", (8, 16, 128), I32),
    ("x_to", (8, ROWS, DIM), BF),
    ("heads_to", (16, 2, 4, 8, 384), BF),
    ("wide_to", (2, 4, 4, 32, WIDE), BF),
    ("out_to", (16, 2, 4, 8, DIM), BF),
    ("hot", (EXPERTS * CAP, ROWS), F32),
    ("slots", ROW_SLOTS, BF),
    ("w_heads", (DIM, 256), BF),
    ("router", (DIM, 128), BF),
    ("a_all", (GTOK, DIM), BF),
    ("pre", (GTOK, 256), F32),
    ("cos", (GTOK, 128), F32),
    ("sin", (GTOK, 128), F32),
    ("qr", (GTOK, 128), BF),
    ("kr", (GTOK, 128), BF),
    ("vv", (GTOK, 128), BF),
    ("mixed", (GTOK, 128), F32),
    ("level", (GTOK, 128), F32),
    ("o_rows", (8, ROWS, 128), BF),
    ("o_to", (8, ROWS, 128), BF),
    ("w_out", (DIM, DIM), BF),
    ("ob", (ROWS, DIM), BF),
    ("x1", (ROWS, DIM), F32),
    ("a2", (ROWS, DIM), BF),
    ("gate", (EXPERTS, ROWS), F32),
    ("gates", (EXPERTS, 8, 128), F32),
    ("gates_to", (EXPERTS, 8, 128), F32),
    ("a2_to", ROW_SLOTS, BF),
    ("a_rows", (EXPERTS * CAP, DIM), BF),
    ("hid", (EXPERTS * CAP, FF), BF),
    ("dy", (EXPERTS * CAP, DIM), BF),
    ("dgu", (EXPERTS * CAP, 2 * FF), BF),
    ("y_rows", ROW_SLOTS, BF),
    ("da_rows", ROW_SLOTS, BF),
    ("grad", (2, 4, 4, 32, WIDE), BF),
    ("grad_mid", (8, 32, WIDE), BF),
    ("stage", (8, CAP, DIM), BF),
    ("sum", (ROWS, DIM), F32),
    ("dgate", (EXPERTS, ROWS), F32),
    ("dl", (128, ROWS), BF),
    ("dx1", (ROWS, DIM), F32),
    ("db", (ROWS, DIM), BF),
    ("do_rows", (8, ROWS, 128), BF),
    ("do_to", (8, ROWS, 128), BF),
    ("gwo_mid", (16, 4, 8, DIM), BF),
    ("gwo_sum", (16, 8, DIM), BF),
    ("gwo_last", (16, 8, DIM), BF),
    ("dq", (GTOK, 128), F32),
    ("dk", (GTOK, 128), F32),
    ("dv", (GTOK, 128), F32),
    ("dqkv", (GTOK, 256), BF),
    ("gain_one_grad", (1, DIM), F32),
    ("gain_q_grad", (1, 128), F32),
    ("gain_k_grad", (1, 128), F32),
    ("side", (DIM, 128), F32),
    ("hg_co", (16, 4, 8, 384), BF),
    ("hg_mid", (16, 4, 8, 384), BF),
    ("hg_z", (4, 16, 8, 384), BF),
    ("hg_sum", (16, 8, 384), BF),
    ("hg_last", (16, 8, 384), BF),
)
SEMS = dict(
    s_stage=1,
    s_picks=8,
    s_x=8,
    s_heads=64,
    s_heads_co=2,
    s_dz=32,
    s_wide=8,
    s_wide_x=4,
    s_out=16,
    s_out_z=4,
    s_out_co=2,
    s_o=8,
    s_a2=32,
    s_gate=32,
    s_y=32,
    s_da=32,
    s_grad=4,
    s_grad_last=8,
    s_do=8,
    s_da1=8,
    s_gwo_co=2,
    s_gwo_z=4,
    s_gwo=16,
    s_hg_co=2,
    s_hg_z=4,
    s_hg=16,
)


def layer(*operands):
    names = [name for name, *_ in INPUTS + OUTPUTS + LANDING + SCRATCH] + list(SEMS)

    def body(*refs):
        layer_kernel(types.SimpleNamespace(**dict(zip(names, refs))))

    return pl.pallas_call(
        body,
        out_shape=[jax.ShapeDtypeStruct(shape, kind) for _, shape, kind in OUTPUTS + LANDING],
        in_specs=[pl.BlockSpec(memory_space=space) for _, space in INPUTS],
        out_specs=[pl.BlockSpec(memory_space=pltpu.VMEM)] * len(OUTPUTS)
        + [pl.BlockSpec(memory_space=pl.ANY)] * len(LANDING),
        scratch_shapes=[pltpu.VMEM(shape, kind) for _, shape, kind in SCRATCH]
        + [pltpu.SemaphoreType.DMA((2, n)) for n in SEMS.values()],
        compiler_params=pltpu.CompilerParams(
            collective_id=0, has_side_effects=True, vmem_limit_bytes=VMEM_LIMIT
        ),
        name="layer",
    )(*operands)


VMEM_LIMIT = 63 << 20


def shards(
    inputs,
    cotangent,
    w_query,
    key_weight,
    value_weight,
    w_output,
    w_router,
    norm_gains,
    w_gate_up,
    w_down,
    seq_lengths,
    block_map,
    routes,
    priority,
):
    heads = jnp.concatenate(
        [
            w_query.reshape(8, 8, 128),
            key_weight.reshape(8, 8, 64),
            value_weight.reshape(8, 8, 64),
            jnp.broadcast_to(w_router[:, None], (8, 8, EXPERTS)),
            jnp.broadcast_to(
                jnp.pad(norm_gains[None, :], ((0, 7), (0, 96 - GAINS)))[:, None], (8, 8, 96)
            ),
        ],
        axis=-1,
    ).transpose(1, 0, 2)
    picks = jnp.concatenate(
        [routes[0].T, priority[0], jnp.zeros((16 - TOPK - 1, ROWS), I32)], axis=0
    )
    wide = jnp.concatenate([w_gate_up, jnp.swapaxes(w_down, 1, 2)], axis=-1)
    output, grad_inputs, head_grad, grad_out, expert_grad, *_ = layer(
        seq_lengths[0], block_map[0], inputs[0], heads, picks, cotangent[0], wide, w_output.T
    )
    expert_grad = expert_grad.astype(F32)
    rows = jnp.swapaxes(head_grad, 0, 1)
    shared = jnp.sum(head_grad, axis=0)
    return (
        output[None],
        grad_inputs[None],
        rows[..., :128].reshape(8, HEADS * HEAD),
        rows[..., 128:192].reshape(8, KV_HEADS * HEAD),
        rows[..., 192:256].reshape(8, KV_HEADS * HEAD),
        grad_out.T,
        shared[:, 256:288],
        shared[0, 288 : 288 + GAINS],
        expert_grad[..., : 2 * FF],
        jnp.swapaxes(expert_grad[..., 2 * FF :], 1, 2),
    )


def solution(mesh):
    groups = ("yh", "co", "z")
    specs = (
        P(groups, CTX, None),
        P(groups, CTX, None),
        P(ALL, None),
        P(ALL, None),
        P(ALL, None),
        P(None, ALL),
        P(ALL, None),
        P(ALL),
        P(("yh", "co"), WT, None),
        P(("yh", "co"), None, WT),
        P(groups, None),
        P(groups, None),
        P(groups, CTX, None),
        P(groups, CTX, None),
    )
    return jax.shard_map(
        shards,
        mesh=Mesh(mesh.devices.reshape(SIZES), ALL),
        in_specs=specs,
        out_specs=specs[:10],
        check_vma=False,
    )
```

profile of v0, /device:TPU:1, one launch (start us, length us, event | category | flops | bytes accessed | tf_op | source)
XLA Modules:
  0.0 274.4 jit_solution(17602487701487471842)
XLA Ops:
  0.7 0.1 pad.9.clone
  0.7 0.7 pad.4
  1.4 1.4 add_add_fusion.refs_4_
  2.8 0.8 reshape.41
  3.6 0.8 reshape.42
  4.3 0.7 broadcast_in_dim.24
  5.0 1.4 concatenate.9
  6.5 2.1 pad_maximum_fusion.refs_6_
  8.5 254.9 %layer.1 = (bf16[128,1024]{1,0:T(8,128)(2,1)}, bf16[128,1024]{1,0:T(8,128)(2,1)}, f32[8,8,384]{2,1,0:T(8,128)}, f32[8,1024]{1,0:T(8,128)}, bf16[8,32,1536]{2,1,0...) custom-call(s32[4]{0:T(128)} %bitcast.35, ...), custom_call_target="tpu_custom_call" | custom-call | tf_op jit(solution)/shard_map/layer/pallas_call | solution.py:784
  263.4 0.0 copy-start
  263.4 1.0 reduce_sum.9
  264.4 0.6 slice_bitcast_fusion.2
  265.0 0.6 slice.31
  265.6 1.4 slice_bitcast_fusion.1
  266.9 0.9 fusion
  267.8 0.7 reshape.45
  268.5 0.7 reshape.44
  269.2 2.1 slice.33
  271.3 0.0 copy-done
  271.3 0.0 copy-start.2
  271.3 0.0 copy-start.1
  271.3 0.2 convert_element_type.5
  271.5 0.0 copy-start.3
  271.5 0.8 slice_bitcast_fusion
  272.4 0.0 copy-done.2
  272.4 0.7 copy.31
  273.1 0.0 copy-done.1
  273.1 0.7 copy.32
  273.8 0.0 copy-done.3
  273.8 0.6 copy.33
  (6 shorter events, 0.0 us)
Async XLA Ops:
  263.4 8.0 %copy-start = (bf16[8,32,1536]{2,1,0:T(8,128)(2,1)S(1)}, bf16[8,32,1536]{2,1,0:T(8,128)(2,1)}, u32[]{:S(2)}) copy-start(bf16[8,32,1536]{2,1,0:T(8,128)(2,1)} %get-tuple-element.19) | copy-start | bytes 2359300
  271.3 1.0 copy-start.2
  271.3 1.7 copy-start.1
  271.5 2.3 copy-start.3
where the time goes:
time: 276 us; the launch traced here: 274 us
  Pallas kernels  255 us (92%)
  local copies, waits for them, and re-layouts  14.3 us (5%)
  other arithmetic  4.59 us (2%)
    pallas_call x1, Pallas kernels, layer(): pl.pallas_call(body, out_shape=[jax.ShapeDtypeStruct(shape, kind) for _,...  255 us

commit v1 on v0

v1 whole, which is shorter than its diff:
```python
import math
import types

import jax
import jax.numpy as jnp
from jax import lax
from jax.experimental import pallas as pl
from jax.experimental.pallas import tpu as pltpu
from jax.sharding import Mesh
from jax.sharding import PartitionSpec as P

HEADS = 16
KV_HEADS = 8
DIM = 1024
HEAD = 64
FF = 512
EXPERTS = 32
TOPK = 8
ROWS = 128
GTOK = 1024
CAP = 40
GAINS = 17
WIDE = 3 * FF
PART = 8 * CAP
BF = jnp.bfloat16
F32 = jnp.float32
I32 = jnp.int32

ALL = ("yl", "x", "yh", "co", "z")
SIZES = (2, 4, 2, 2, 4)
SPAN = dict(zip(ALL, SIZES))
CTX = ("yl", "x")
EP = ("yh", "co", "yl", "z")
WT = ("yl", "x", "z")
LONG = ("yl", "x", "yh")
FLAT = ("yl", "yh", "z")


def linear(axes):
    index = 0
    for axis in axes:
        index = index * SPAN[axis] + lax.axis_index(axis)
    return index


def spin(axis, step):
    at = lax.axis_index(axis)
    return at if isinstance(step, int) and step == 0 else lax.rem(at + step, SPAN[axis])


def partner(axes, i):
    steps, at, index = {}, {}, 0
    for axis in reversed(axes):
        if isinstance(i, int):
            steps[axis], i = i % SPAN[axis], i // SPAN[axis]
        else:
            steps[axis], i = lax.rem(i, SPAN[axis]), lax.div(i, SPAN[axis])
    for axis in axes:
        at[axis] = spin(axis, steps[axis])
        index = index * SPAN[axis] + at[axis]
    return index, tuple(at[axis] if axis in at else lax.axis_index(axis) for axis in ALL)


def count(axes):
    return math.prod(SPAN[axis] for axis in axes)


def greet(sets, meanwhile):
    barrier = pltpu.get_barrier_semaphore()
    for axes in sets:
        for i in range(1, count(axes)):
            pl.semaphore_signal(
                barrier,
                inc=1,
                device_id=partner(axes, i)[1],
                device_id_type=pl.DeviceIdType.MESH,
            )
    meanwhile()
    pl.semaphore_wait(barrier, sum(count(axes) - 1 for axes in sets))


def remote(source, target, send_sem, recv_sem, to):
    return pltpu.make_async_remote_copy(
        src_ref=source,
        dst_ref=target,
        send_sem=send_sem,
        recv_sem=recv_sem,
        device_id=to,
        device_id_type=pl.DeviceIdType.MESH,
    )


def drain(span, sem):
    pltpu.make_async_copy(span, span, sem).wait()


class Send:
    def __init__(self, axes, part, slot, slots, sems, own=True):
        self.axes, self.part, self.slot, self.slots = axes, part, slot, slots
        self.sems, self.own, self.n, self.me = sems, own, count(axes), linear(axes)

    def copy(self, i, arrival=1, departure=0):
        place, to = partner(self.axes, i)
        send_sem, recv_sem = self.sems.at[departure], self.sems.at[arrival]
        return remote(self.part(place), self.slot(self.me), send_sem, recv_sem, to)

    def start_own(self, arrival=1):
        pltpu.make_async_copy(
            self.part(self.me), self.slot(self.me), self.sems.at[arrival]
        ).start()

    def start(self):
        if self.own:
            self.start_own()
        for i in range(1, self.n):
            self.copy(i).start()

    def arrived(self):
        drain(self.slots(self.n if self.own else self.n - 1), self.sems.at[1])

    def sent(self):
        drain(self.slots(self.n - 1), self.sems.at[0])

    def wait(self):
        self.arrived()
        self.sent()


class Pairs:
    def __init__(self, blocks, landing, sems):
        self.blocks, self.landing, self.sems, self.me = blocks, landing, sems, linear(EP)

    def start(self, c):
        yh, co = spin("yh", lax.div(c, 2)), spin("co", lax.rem(c, 2))
        for j in range(8):
            yl, z = spin("yl", j // 4), spin("z", j % 4)
            place = ((yh * 2 + co) * 2 + yl) * 4 + z
            copy = remote(
                self.blocks.at[place],
                self.landing.at[self.me],
                self.sems.at[4 + c],
                self.sems.at[c],
                (yl, lax.axis_index("x"), yh, co, z),
            )
            if j > 0:
                copy.start()
                continue

            @pl.when(c > 0)
            def _(copy=copy):
                copy.start()

            @pl.when(c == 0)
            def _():
                pltpu.make_async_copy(
                    self.blocks.at[self.me], self.landing.at[self.me], self.sems.at[0]
                ).start()

    def start_all(self):
        def one(c, carry):
            self.start(c)
            return carry

        lax.fori_loop(0, 4, one, 0)

    def arrived(self, c):
        drain(self.landing.at[pl.ds(0, 8)], self.sems.at[c])

    def sent(self, c):
        @pl.when(c > 0)
        def _():
            drain(self.blocks.at[pl.ds(0, 8)], self.sems.at[4 + c])

        @pl.when(c == 0)
        def _():
            drain(self.blocks.at[pl.ds(0, 7)], self.sems.at[4])

    def all_sent(self):
        def one(c, carry):
            self.sent(c)
            return carry

        lax.fori_loop(0, 4, one, 0)


def dot(left, right, dims=((1,), (0,))):
    return lax.dot_general(left, right, (dims, ((), ())), preferred_element_type=F32)


def rms(v):
    return lax.rsqrt(jnp.mean(v * v, axis=-1, keepdims=True) + 1e-06)


def norm_back(v, scale, gain, upstream):
    weighted = upstream * gain
    inner = jnp.mean(weighted * v, axis=-1, keepdims=True)
    return scale * weighted - v * (scale * scale * scale) * inner, upstream * v * scale


def halves():
    lane = lax.broadcasted_iota(I32, (1, 128), 1)
    return lane < HEAD, lax.rem(lane, HEAD) < HEAD // 2


def head_mean(v, first):
    low = jnp.sum(jnp.where(first, v, 0.0), axis=1, keepdims=True)
    high = jnp.sum(jnp.where(first, 0.0, v), axis=1, keepdims=True)
    return jnp.where(first, low, high) * (1.0 / HEAD)


def head_rms(v, first):
    return lax.rsqrt(head_mean(v * v, first) + 1e-06)


def head_norm_back(v, gain, upstream, first):
    scale = head_rms(v, first)
    weighted = upstream * gain
    inner = head_mean(weighted * v, first)
    terms = jnp.sum(upstream * v * scale, axis=0, keepdims=True)
    return scale * weighted - v * (scale * scale * scale) * inner, terms


def turn_pair(v, cos, sin, front):
    return v * cos + jnp.where(front, -pltpu.roll(v, 96, 1), pltpu.roll(v, 32, 1)) * sin


def starts(tokens, ends):
    first = jnp.zeros_like(tokens)
    for end in ends:
        first = jnp.maximum(first, jnp.where(tokens >= end, end, 0))
    return first


def sequence_ends(lengths):
    ends, total = [], 0
    for i in range(3):
        total = total + lengths[i]
        ends.append(total)
    return ends


def gain_places():
    column = lax.broadcasted_iota(I32, (128, 128 * GAINS), 1)
    row = lax.broadcasted_iota(I32, (128, 128 * GAINS), 0)
    owner = (column * 3856) >> 16
    return row == owner, row == EXPERTS + column - owner * GAINS


def spread_gains(packed):
    owner, lane = gain_places()
    rows = dot(packed, owner.astype(F32).astype(BF), ((0,), (0,)))
    return jnp.sum(jnp.where(lane, rows, 0.0), axis=0, keepdims=True)


def pack_gains(row):
    owner, lane = gain_places()
    return dot(
        owner.astype(F32).astype(BF), jnp.where(lane, row, 0.0).astype(BF), ((1,), (1,))
    )


def merge(v):
    shape = v.shape
    return v.astype(F32).reshape(math.prod(shape[:-1]), shape[-1]).astype(BF)


def rows_of(j):
    return pl.ds(j * ROWS if isinstance(j, int) else pl.multiple_of(j * ROWS, ROWS), ROWS)


def layer_kernel(r):
    def pack():
        wq, wk, wv, wr, gains = (
            ref[...].astype(F32) for ref in (r.wq, r.wk, r.wv, r.wr, r.norm)
        )
        gains = jnp.concatenate([gains, jnp.zeros((7, GAINS), F32)], axis=0)
        side = jnp.concatenate([wr, gains, jnp.zeros((8, 96 - GAINS), F32)], axis=1)
        for h in range(8):
            at = slice(h * HEAD, (h + 1) * HEAD)
            row = [wq[:, h * 128 : (h + 1) * 128], wk[:, at], wv[:, at], side]
            row = jnp.concatenate(row, axis=1).astype(BF)
            r.heads[h] = row
            r.wall[:, h * 256 : (h + 1) * 256] = row[:, :256]
        r.picks[pl.ds(0, 8)] = r.routes[...]
        r.picks[pl.ds(8, 8)] = jnp.broadcast_to(r.priority[...], (8, ROWS))

    greet((EP, LONG), pack)
    place = linear(CTX)
    spot, core, deep = lax.axis_index("x"), lax.axis_index("co"), lax.axis_index("z")
    yl, yh = lax.axis_index("yl"), lax.axis_index("yh")
    first, front = halves()

    def bring(source, target):
        copy = pltpu.make_async_copy(source, target, r.s_stage.at[0])
        copy.start()
        return copy

    send_picks = Send(
        CTX, lambda p: r.picks, lambda q: r.picks_to.at[q], lambda n: r.picks_to.at[pl.ds(0, n)], r.s_picks
    )
    cross_x = Send(
        ("yl",), lambda p: r.x, lambda q: r.x_to.at[q * 4 + spot], lambda n: r.x, r.s_x, own=False
    )
    send_x = Send(
        ("x",), lambda p: r.x, lambda q: r.x_to.at[yl * 4 + q], lambda n: r.x_to.at[pl.ds(0, n)], r.s_x
    )
    pass_x = Send(
        ("x",),
        lambda p: r.x_to.at[(1 - yl) * 4 + spot],
        lambda q: r.x_to.at[(1 - yl) * 4 + q],
        lambda n: r.x_to.at[pl.ds(0, n)],
        r.s_x,
    )
    send_heads = Send(
        CTX,
        lambda p: r.heads.at[p],
        lambda q: r.heads_to.at[q, yh, core, deep],
        lambda n: r.heads_to.at[pl.ds(0, n), yh, core, deep],
        r.s_heads,
    )
    pass_heads = Send(
        ("yh", "z"),
        lambda p: r.heads_to.at[:, yh, core, deep],
        lambda q: r.heads_to.at[:, lax.div(q, 4), core, lax.rem(q, 4)],
        lambda n: r.heads_to.at[pl.ds(0, n), :, :, pl.ds(0, 2)],
        r.s_heads_pass,
        own=False,
    )
    swap_heads = Send(
        ("co",),
        lambda p: r.heads_to.at[:, :, core],
        lambda q: r.heads_to.at[:, :, q],
        lambda n: r.heads_to.at[:, :, 0],
        r.s_heads_co,
        own=False,
    )
    send_gu = Send(
        ("yl", "z"),
        lambda p: r.w_gu.at[p],
        lambda q: r.wide_to.at[lax.div(q, 4), spot, lax.rem(q, 4), :, pl.ds(0, 2 * FF)],
        lambda n: r.w_gu.at[pl.ds(0, n)],
        r.s_gu,
    )
    send_dn = Send(
        ("yl", "z"),
        lambda p: r.w_dn.at[p],
        lambda q: r.wide_to.at[lax.div(q, 4), spot, lax.rem(q, 4), :, pl.ds(2 * FF, FF)],
        lambda n: r.w_dn.at[pl.ds(0, n)],
        r.s_dn,
    )
    pass_wide = Send(
        ("x",),
        lambda p: r.wide_to.at[:, spot],
        lambda q: r.wide_to.at[:, q],
        lambda n: r.wide_to.at[:, pl.ds(0, n)],
        r.s_wide,
        own=False,
    )
    send_out = Send(
        LONG,
        lambda p: r.out,
        lambda q: r.out_to.at[q, core, deep],
        lambda n: r.out_to.at[pl.ds(0, n), core, deep],
        r.s_out,
    )
    pass_out = Send(
        ("z",),
        lambda p: r.out_to.at[:, core, deep],
        lambda q: r.out_to.at[:, core, q],
        lambda n: r.out_to.at[:, core, pl.ds(0, n)],
        r.s_out_z,
        own=False,
    )
    swap_out = Send(
        ("co",),
        lambda p: r.out_to.at[:, core],
        lambda q: r.out_to.at[:, q],
        lambda n: r.out_to.at[:, 0],
        r.s_out_co,
        own=False,
    )
    send_all = Send(
        FLAT,
        lambda p: r.wall,
        lambda q: r.wall_to.at[q, spot, core],
        lambda n: r.wall_to.at[pl.ds(0, n), 0, 0],
        r.s_all,
    )
    pass_all = Send(
        ("x",),
        lambda p: r.wall_to.at[:, spot, core],
        lambda q: r.wall_to.at[:, q, core],
        lambda n: r.wall_to.at[:, pl.ds(0, n), core],
        r.s_all_x,
        own=False,
    )
    swap_all = Send(
        ("co",),
        lambda p: r.wall_to.at[:, :, core],
        lambda q: r.wall_to.at[:, :, q],
        lambda n: r.wall_to.at[:, :, 0],
        r.s_all_co,
        own=False,
    )
    send_o = Send(
        CTX, lambda p: r.o_rows.at[p], lambda q: r.o_to.at[q], lambda n: r.o_to.at[pl.ds(0, n)], r.s_o
    )
    send_dz = Pairs(r.dz_rows, r.dz_to, r.s_dz)
    send_a2 = Pairs(r.a2_rows, r.a2_to, r.s_a2)
    send_gate = Pairs(r.gates, r.gates_to, r.s_gate)
    send_da = Pairs(r.a2_rows, r.da_to, r.s_da)
    send_dg = Pairs(r.dg_rows, r.dg_to, r.s_dg)
    send_y = Pairs(r.dz_rows, r.y_to, r.s_y)
    send_grad = Send(
        ("x",),
        lambda p: r.grad.at[:, p],
        lambda q: r.grad_to.at[:, q],
        lambda n: r.grad.at[:, pl.ds(0, n)],
        r.s_grad,
    )
    last_grad = Send(
        ("yl", "z"),
        lambda p: r.grad_mid.at[p],
        lambda q: r.grad_last.at[q],
        lambda n: r.grad_mid.at[pl.ds(0, n)],
        r.s_grad_last,
    )
    send_do = Send(
        CTX, lambda p: r.do_rows.at[p], lambda q: r.do_to.at[q], lambda n: r.do_to.at[pl.ds(0, n)], r.s_do
    )
    send_dq = Send(
        CTX,
        lambda p: r.dqkv.at[rows_of(p)],
        lambda q: r.dq_to.at[q],
        lambda n: r.dq_to.at[pl.ds(0, n)],
        r.s_dq,
    )
    swap_gwo = Send(
        ("co",), lambda p: r.out_to.at[:, p], lambda q: r.gwo_co, lambda n: r.gwo_co, r.s_gwo_co, own=False
    )
    pass_gwo = Send(
        ("x",),
        lambda p: r.gwo_mid.at[:, p],
        lambda q: r.gwo_x.at[:, q],
        lambda n: r.gwo_x.at[:, pl.ds(0, n)],
        r.s_gwo_x,
    )
    last_gwo = Send(
        FLAT,
        lambda p: r.gwo_sum.at[p],
        lambda q: r.gwo_last.at[q],
        lambda n: r.gwo_sum.at[pl.ds(0, n)],
        r.s_gwo,
    )
    swap_hg = Send(
        ("co",),
        lambda p: r.heads_to.at[:, :, p],
        lambda q: r.hg_co,
        lambda n: r.hg_co,
        r.s_hg_co,
        own=False,
    )
    pass_hg = Send(
        ("z",),
        lambda p: r.hg_mid.at[:, :, p],
        lambda q: r.hg_z.at[q],
        lambda n: r.hg_z.at[pl.ds(0, n)],
        r.s_hg_z,
    )
    last_hg = Send(
        LONG,
        lambda p: r.hg_sum.at[lax.div(p, 2), lax.rem(p, 2)],
        lambda q: r.hg_last.at[q],
        lambda n: r.hg_last.at[pl.ds(0, n)],
        r.s_hg,
    )

    send_picks.start()
    cross_x.copy(1, 4, 8).start()
    send_x.start_own(0)
    for i in range(1, 4):
        send_x.copy(i, i, 9).start()
    send_heads.start()
    send_out.start()
    send_gu.start()
    send_dn.start()

    send_picks.wait()
    mine = jnp.zeros((16, 128), I32)
    for p in range(8):
        mine = mine + r.picks_to[p] * (r.blocks[p] == place).astype(I32)
    expert = lax.broadcasted_iota(I32, (EXPERTS, ROWS), 0)
    named = jnp.zeros((EXPERTS, ROWS), jnp.bool_)
    for k in range(TOPK):
        named = named | (mine[k : k + 1] == expert)
    order = jnp.broadcast_to(mine[TOPK : TOPK + 1].astype(F32), (128, ROWS))
    before = (order.T < order).astype(F32).astype(BF)
    rank = jnp.where(named, dot(named.astype(F32).astype(BF), before), -1.0)
    seat = lax.broadcasted_iota(I32, (CAP, ROWS), 0).astype(F32)
    for e in range(EXPERTS):
        r.hot[pl.ds(e * CAP, CAP)] = (rank[e : e + 1] == seat).astype(F32)

    def part_of(c):
        return spin("yh", lax.div(c, 2)) * 2 + spin("co", lax.rem(c, 2))

    def fill(source, rows, c):
        for i in range(2):
            eight = part_of(c) * 8 + 4 * i
            at = pl.ds(pl.multiple_of(eight * CAP, 4 * CAP), 4 * CAP)
            part = dot(r.hot[at].astype(BF), source[...])
            rows[pl.ds(eight, 4)] = part.reshape(4, CAP, DIM).astype(BF)

    drain(r.x, r.s_x.at[4])
    for i in range(1, 4):
        pass_x.copy(i, 4 + i, 10).start()
    send_heads.wait()
    pass_heads.start()
    send_out.wait()
    pass_out.start()
    pass_heads.wait()
    swap_heads.start()

    def fill_dz(c, carry):
        fill(r.dz, r.dz_rows, c)
        send_dz.start(c)
        return carry

    lax.fori_loop(0, 4, fill_dz, 0)
    swap_heads.wait()

    packed = r.heads_to[...].astype(F32).reshape(128, 8, 384)
    r.w_heads[...] = packed[:, :, :256].reshape(DIM, 256).astype(BF)
    r.router[...] = packed[:, :, 256:].reshape(DIM, 128).astype(BF)
    gains = spread_gains(packed[:, 0, 256:].astype(BF))
    gain_one, gain_two, pair = gains[:, :DIM], gains[:, DIM : 2 * DIM], gains[:, 2 * DIM :]
    swapped = pltpu.roll(pair, HEAD, 1)
    gain_q, gain_k = jnp.where(first, pair, swapped), jnp.where(first, swapped, pair)
    ends = sequence_ends(r.lengths)
    lane = lax.broadcasted_iota(I32, (1, 128), 1)
    frequency = jnp.exp(
        lax.rem(lane, HEAD // 2).astype(F32) * (-2.0 * math.log(10000.0) / HEAD)
    )

    def project(j):
        at = rows_of(j)
        v = r.x_to[j].astype(F32)
        low = (v * rms(v) * gain_one).astype(BF)
        r.a_all[at] = low
        qkv = dot(low, r.w_heads[...])
        r.pre[at] = qkv
        token = j * ROWS + lax.broadcasted_iota(I32, (ROWS, 1), 0)
        angle = (token - starts(token, ends)).astype(F32) * frequency
        cos, sin = jnp.cos(angle), jnp.sin(angle)
        r.cos[at] = cos
        r.sin[at] = sin
        q, kv = qkv[:, :128], qkv[:, 128:]
        other = pltpu.roll(kv, HEAD, 1)
        k, val = jnp.where(first, kv, other), jnp.where(first, other, kv)
        r.qr[at] = turn_pair(q * head_rms(q, first) * gain_q, cos, sin, front).astype(BF)
        r.kr[at] = turn_pair(k * head_rms(k, first) * gain_k, cos, sin, front).astype(BF)
        r.vv[at] = val.astype(BF)

    def arrive(i, carry):
        @pl.when(i != 4)
        def _():
            drain(r.x, r.s_x.at[i])

        project(spin("yl", 2 - lax.div(i, 4)) * 4 + spin("x", 4 - lax.rem(i, 4)))
        return carry

    lax.fori_loop(0, 8, arrive, 0)
    drain(r.x, r.s_x.at[8])
    for n in (9, 10):
        drain(send_x.slots(3), r.s_x.at[n])
    send_gu.wait()
    send_dn.wait()
    pass_wide.start()
    send_all.start()

    def stacked(v):
        v = v.astype(F32)
        return jnp.concatenate(
            [jnp.where(first, v, 0.0), jnp.where(first, 0.0, v)], axis=0
        ).astype(BF)

    def beside(v):
        return jnp.where(first, v[:ROWS], v[ROWS:])

    def masked_scores(tile, q, width):
        scores = dot(q, r.kr[pl.ds(0, width)], ((1,), (1,))) * HEAD**-0.5
        token = tile * ROWS + lax.rem(lax.broadcasted_iota(I32, (2 * ROWS, 1), 0), ROWS)
        key = lax.broadcasted_iota(I32, (2 * ROWS, width), 1)
        return jnp.where((key <= token) & (key >= starts(token, ends)), scores, -1e30)

    for tile in range(8):
        width, at = ROWS * (tile + 1), rows_of(tile)
        scores = masked_scores(tile, stacked(r.qr[at]), width)
        top = jnp.max(scores, axis=1, keepdims=True)
        weight = jnp.exp(scores - top)
        total = jnp.sum(weight, axis=1, keepdims=True)
        result = beside(dot((weight * (1.0 / total)).astype(BF), r.vv[pl.ds(0, width)]))
        r.mixed[at] = result
        r.o_rows[tile] = result.astype(BF)
        r.level[at] = beside(jnp.broadcast_to(top + jnp.log(total), (2 * ROWS, 128)))
    send_o.start()
    pass_out.wait()
    swap_out.start()
    swap_out.wait()

    def lay(i, carry):
        r.w_out[rows_of(i)] = merge(r.out_to[pl.ds(2 * i, 2)])
        return carry

    lax.fori_loop(0, 8, lay, 0)

    send_o.wait()
    for h in range(8):
        r.ob[:, h * 128 : (h + 1) * 128] = r.o_to[h]
    x_own = r.x[...].astype(F32)
    dz = r.dz[...].astype(F32)
    x1 = x_own + dot(r.ob[...], r.w_out[...], ((1,), (1,)))
    r.x1[...] = x1
    r2 = rms(x1)
    r.a2[...] = (x1 * r2 * gain_two).astype(BF)
    logits = dot(r.router[...], r.a2[...], ((0,), (1,)))[:EXPERTS]
    weight = jnp.exp(logits - jnp.max(logits, axis=0, keepdims=True))
    probs = weight / jnp.sum(weight, axis=0, keepdims=True)
    chosen = jnp.where(named, probs, 0.0)
    total = jnp.sum(chosen, axis=0, keepdims=True)
    gate = chosen / total
    r.gate[...] = gate
    r.gates[:, 0, :] = gate
    r.gates[:, 1, :] = rank
    send_gate.start_all()

    def fill_a2(c, carry):
        fill(r.a2, r.a2_rows, c)
        send_a2.start(c)
        return carry

    lax.fori_loop(0, 4, fill_a2, 0)
    send_all.wait()
    pass_all.start()
    pass_wide.wait()

    send_dz.all_sent()
    w_all = r.wide_to.reshape(DIM, WIDE)
    w_gu, w_dn = w_all.at[:, : 2 * FF], w_all.at[:, 2 * FF :]

    def work(c, carry):
        send_gate.arrived(c)
        send_dz.arrived(c)
        k8 = part_of(c) * 8
        at = pl.ds(pl.multiple_of(c * PART, PART), PART)
        staged = bring(r.dz_to.at[pl.ds(k8, 8)], r.stage)
        send_a2.arrived(c)
        a = merge(r.a2_to[pl.ds(k8, 8)])
        r.a_rows[at] = a
        gu = dot(a, w_gu[...])
        g, up = gu[:, :FF], gu[:, FF:]
        s = 1.0 / (1.0 + jnp.exp(-g))
        hid = (g * s * up).astype(BF)
        r.hid[at] = hid
        note = r.gates_to[pl.ds(k8, 8)]
        kept = note[:, 1:2] == seat[None]
        column = jnp.sum(jnp.where(kept, note[:, 0:1], 0.0), axis=2, keepdims=True)
        staged.wait()
        dz_part = r.stage[...].astype(F32)
        dy = (dz_part * column).reshape(PART, DIM).astype(BF)
        r.dy[at] = dy
        dhid = dot(dy, w_dn[...])
        dgu = jnp.concatenate([dhid * up * s * (1.0 + g * (1.0 - s)), dhid * g * s], axis=1)
        dgu = dgu.astype(BF)
        r.dgu[at] = dgu
        da = dot(dgu, w_gu[...], ((1,), (1,)))
        send_a2.sent(c)
        r.a2_rows[pl.ds(k8, 8)] = da.reshape(8, CAP, DIM).astype(BF)
        send_da.start(c)
        y = dot(hid, w_dn[...], ((1,), (1,))).reshape(8, CAP, DIM).astype(BF)
        r.dz_rows[pl.ds(k8, 8)] = y
        inner = jnp.sum(y.astype(F32) * dz_part, axis=2, keepdims=True)
        inner = jnp.sum(jnp.where(kept, inner, 0.0), axis=1, keepdims=True)
        r.dg_rows[pl.ds(k8, 8)] = jnp.broadcast_to(inner, (8, 8, ROWS))
        send_dg.start(c)
        return carry

    lax.fori_loop(0, 4, work, 0)

    def weigh(i, carry):
        to = spin("x", i)
        for half in range(2):
            at = rows_of(half * 4 + to)
            gu = dot(r.a_rows[:, at], r.dgu[...], ((0,), (0,)))
            r.grad[half, to, :, :, : 2 * FF] = gu.astype(BF).reshape(4, 32, 2 * FF)
            dn = dot(r.dy[:, at], r.hid[...], ((0,), (0,)))
            r.grad[half, to, :, :, 2 * FF :] = dn.astype(BF).reshape(4, 32, FF)

        @pl.when(i < 4)
        def _():
            send_grad.copy(i).start()

        return carry

    lax.fori_loop(1, 5, weigh, 0)
    send_grad.start_own()

    pass_all.wait()
    swap_all.start()
    for c in range(4):
        send_dg.arrived(c)
    dgate = r.dg_to[:, 0, :]
    dc = jnp.where(named, dgate - jnp.sum(gate * dgate, axis=0, keepdims=True), 0.0) / total
    dl = probs * (dc - jnp.sum(probs * dc, axis=0, keepdims=True))
    dl = jnp.concatenate([dl, jnp.zeros((128 - EXPERTS, ROWS), F32)], axis=0).astype(BF)
    r.dl[...] = dl
    r.sum[...] = dot(dl, r.router[...], ((0,), (1,)))

    def hot_part(c):
        return r.hot[pl.ds(pl.multiple_of(part_of(c) * PART, PART), PART)]

    def unmix(c, carry):
        send_da.arrived(c)
        bring(r.da_to.at[pl.ds(part_of(c) * 8, 8)], r.stage).wait()
        r.sum[...] += dot(hot_part(c).astype(BF), merge(r.stage[...]), ((0,), (0,)))
        return carry

    lax.fori_loop(0, 4, unmix, 0)
    dx_two, terms_two = norm_back(r.x1[...], rms(r.x1[...]), gain_two, r.sum[...])
    gain_two_grad = jnp.sum(terms_two, axis=0, keepdims=True)
    r.dx1[...] = dz + dx_two
    r.db[...] = r.dx1[...].astype(BF)
    do = dot(r.db[...], r.w_out[...]).astype(BF)
    for h in range(8):
        r.do_rows[h] = do[:, h * 128 : (h + 1) * 128]
    send_do.start()

    send_y.start(0)
    send_y.start(1)

    def spread_out(i, carry):
        part = dot(r.db[:, rows_of(i)], r.ob[...], ((0,), (0,)))
        part = part.reshape(2, 2, 4, 8, DIM).astype(BF)
        for n in range(4):
            at = pl.ds((lax.div(i, 4) * 2 + n // 2) * 4, 4)
            r.out_to[at, n % 2, lax.rem(i, 4)] = part[n // 2, n % 2]
        return carry

    lax.fori_loop(0, 8, spread_out, 0)
    swap_gwo.start()

    def add_core(i, carry):
        both = r.gwo_mid[i].astype(F32) + r.out_to[i, core].astype(F32)
        r.gwo_mid[i] = both.astype(BF)
        return carry

    send_do.wait()
    r.dk[...] = jnp.zeros_like(r.dk)
    r.dv[...] = jnp.zeros_like(r.dv)
    for tile in range(8):
        width, at = ROWS * (tile + 1), rows_of(tile)
        keys = pl.ds(0, width)
        q = stacked(r.qr[at])
        level = r.level[at]
        level = jnp.concatenate([level[:, :1], level[:, HEAD : HEAD + 1]], axis=0)
        probs_at = jnp.exp(masked_scores(tile, q, width) - level)
        do = r.do_to[tile]
        inner = head_mean(do.astype(F32) * r.mixed[at], first) * HEAD
        inner = jnp.concatenate([inner[:, :1], inner[:, HEAD : HEAD + 1]], axis=0)
        do = stacked(do)
        dp = dot(do, r.vv[keys], ((1,), (1,)))
        ds = (probs_at * (dp - inner)).astype(BF)
        r.dq[at] = beside(dot(ds, r.kr[keys])) * HEAD**-0.5
        r.dk[keys] += dot(ds, q, ((0,), (0,)))
        r.dv[keys] += dot(probs_at.astype(BF), do, ((0,), (0,)))

    swap_gwo.wait()
    bring(r.gwo_co, r.gwo_mid).wait()
    lax.fori_loop(0, 16, add_core, 0)
    pass_gwo.start()
    r.gain_q_grad[...] = jnp.zeros_like(r.gain_q_grad)
    r.gain_k_grad[...] = jnp.zeros_like(r.gain_k_grad)

    def back(i, carry):
        j, _ = partner(CTX, lax.rem(i, 8))
        at = rows_of(j)
        cos, sin = r.cos[at], -r.sin[at]
        qkv = r.pre[at]
        q, kv = qkv[:, :128], qkv[:, 128:]
        k = jnp.where(first, kv, pltpu.roll(kv, HEAD, 1))
        dk, dv = r.dk[at] * HEAD**-0.5, r.dv[at]
        dk, dv = dk + pltpu.roll(dk, HEAD, 1), dv + pltpu.roll(dv, HEAD, 1)
        dq, terms = head_norm_back(q, gain_q, turn_pair(r.dq[at], cos, sin, front), first)
        r.gain_q_grad[...] += terms
        dk, terms = head_norm_back(k, gain_k, turn_pair(dk, cos, sin, front), first)
        r.gain_k_grad[...] += terms
        r.dqkv[at] = jnp.concatenate([dq, jnp.where(first, dk, dv)], axis=1).astype(BF)

        @pl.when(i < 8)
        def _():
            send_dq.copy(i).start()

        return carry

    lax.fori_loop(1, 9, back, 0)
    send_dq.start_own()

    diagonal = lax.broadcasted_iota(I32, (ROWS, 128), 0) == lax.broadcasted_iota(I32, (ROWS, 128), 1)

    def small(i, carry):
        at = rows_of(i)
        part = dot(r.a_all[:, at], r.dqkv[...], ((0,), (0,)))
        r.heads_to[i, :, :, :, :, pl.ds(0, 256)] = part.reshape(2, 2, 4, 8, 256).astype(BF)
        column = jnp.sum(part * r.w_heads[at].astype(F32), axis=1, keepdims=True)
        r.gain_one_grad[:, at] = jnp.sum(jnp.where(diagonal, column, 0.0), axis=0, keepdims=True)
        return carry

    lax.fori_loop(0, 8, small, 0)
    pair = jnp.where(
        first,
        r.gain_q_grad[...] + pltpu.roll(r.gain_q_grad[...], HEAD, 1),
        r.gain_k_grad[...],
    )
    gain_grads = pack_gains(
        jnp.concatenate([r.gain_one_grad[...] / gain_one, gain_two_grad, pair], axis=1)
    )
    side = jnp.where(
        lax.broadcasted_iota(I32, (128, 8, 128), 1) == 0, gain_grads[:, None], 0.0
    ).reshape(DIM, 128) + dot(r.a2[...], r.dl[...], ((0,), (1,)))
    r.heads_to[:, :, :, :, :, pl.ds(256, 128)] = side.reshape(8, 2, 2, 4, 8, 128).astype(BF)
    swap_hg.start()

    send_grad.wait()
    bring(r.grad_to, r.wide_to).wait()

    def add_grad(i, carry):
        total = sum(r.wide_to[lax.div(i, 4), n, lax.rem(i, 4)].astype(F32) for n in range(4))
        r.grad_mid[i] = total.astype(BF)
        return carry

    lax.fori_loop(0, 8, add_grad, 0)
    last_grad.start()
    swap_hg.wait()
    r.hg_mid[...] = (r.heads_to[:, :, core].astype(F32) + r.hg_co[...].astype(F32)).astype(BF)
    pass_hg.start()
    send_y.start(2)
    send_y.start(3)
    pass_gwo.wait()
    bring(r.gwo_x, r.out_to.at[:, 0]).wait()

    def add_spot(i, carry):
        total = sum(r.out_to[i, 0, n].astype(F32) for n in range(4))
        r.gwo_sum[i] = total.astype(BF)
        return carry

    lax.fori_loop(0, 16, add_spot, 0)
    last_gwo.start()
    pass_hg.wait()
    r.hg_sum[...] = sum(r.hg_z[n].astype(F32) for n in range(4)).astype(BF)
    last_hg.start()

    send_dq.wait()
    swap_all.wait()
    for h in range(8):
        r.dq_all[:, h * 256 : (h + 1) * 256] = r.dq_to[h]

    def fetch(i):
        for n in range(4):
            pltpu.make_async_copy(
                r.wall_to.at[pl.ds((lax.div(i, 4) * 2 + n // 2) * 4, 4), lax.rem(i, 4), n % 2],
                r.wall_rows.at[lax.rem(i, 2), pl.ds(4 * n, 4)],
                r.s_fetch.at[lax.rem(i, 2)],
            ).start()

    fetch(0)

    def unproject(i, carry):
        @pl.when(i < 7)
        def _():
            fetch(i + 1)

        now = lax.rem(i, 2)
        drain(r.wall_rows.at[now], r.s_fetch.at[now])
        r.sum[:, rows_of(i)] = dot(r.dq_all[...], merge(r.wall_rows[now]), ((1,), (1,)))
        return carry

    lax.fori_loop(0, 8, unproject, 0)
    x_own = r.x[...].astype(F32)
    dx_one, _ = norm_back(x_own, rms(x_own), gain_one, r.sum[...])
    r.grad_inputs[...] = (r.dx1[...] + dx_one).astype(BF)

    r.sum[...] = r.x1[...]

    def mix(c, carry):
        send_y.arrived(c)
        k8 = pl.multiple_of(part_of(c) * 8, 8)
        bring(r.y_to.at[pl.ds(k8, 8)], r.stage).wait()
        y = merge(r.stage[...])
        weights = hot_part(c).reshape(8, CAP, ROWS) * r.gate[pl.ds(k8, 8)][:, None]
        weights = weights.reshape(PART, ROWS)
        high = weights.astype(BF)
        low = (weights - high.astype(F32)).astype(BF)
        r.sum[...] += dot(high, y, ((0,), (0,))) + dot(low, y, ((0,), (0,)))
        return carry

    lax.fori_loop(0, 4, mix, 0)
    r.output[...] = r.sum[...].astype(BF)
    for send in (last_gwo, last_grad, last_hg):
        send.wait()
    for send in (send_gate, send_da, send_dg, send_y):
        send.all_sent()


INPUTS = (
    ("lengths", pltpu.SMEM),
    ("blocks", pltpu.SMEM),
    ("x", pltpu.VMEM),
    ("dz", pltpu.VMEM),
    ("wq", pltpu.VMEM),
    ("wk", pltpu.VMEM),
    ("wv", pltpu.VMEM),
    ("wr", pltpu.VMEM),
    ("norm", pltpu.VMEM),
    ("out", pltpu.VMEM),
    ("routes", pltpu.VMEM),
    ("priority", pltpu.VMEM),
    ("w_gu", pl.ANY),
    ("w_dn", pl.ANY),
)
OUTPUTS = (
    ("output", (ROWS, DIM), BF),
    ("grad_inputs", (ROWS, DIM), BF),
)
ROW_SLOTS = (EXPERTS, CAP, DIM)
LANDING = (
    ("hg_last", (16, 8, 384), BF),
    ("gwo_last", (16, 8, DIM), BF),
    ("grad_last", (8, 32, WIDE), BF),
    ("dz_to", ROW_SLOTS, BF),
    ("y_to", ROW_SLOTS, BF),
    ("da_to", ROW_SLOTS, BF),
    ("grad_to", (2, 4, 4, 32, WIDE), BF),
    ("gwo_co", (16, 4, 8, DIM), BF),
    ("gwo_x", (16, 4, 8, DIM), BF),
    ("wall_to", (16, 4, 2, 8, 2 * DIM), BF),
)
SCRATCH = (
    ("heads", (8, 8, 384), BF),
    ("picks", (16, 128), I32),
    ("picks_to", (8, 16, 128), I32),
    ("x_to", (8, ROWS, DIM), BF),
    ("heads_to", (8, 2, 2, 4, 8, 384), BF),
    ("wide_to", (2, 4, 4, 32, WIDE), BF),
    ("out_to", (16, 2, 4, 8, DIM), BF),
    ("hot", (EXPERTS * CAP, ROWS), F32),
    ("wall", (8, 2 * DIM), BF),
    ("dz_rows", ROW_SLOTS, BF),
    ("a2_rows", ROW_SLOTS, BF),
    ("w_heads", (DIM, 256), BF),
    ("router", (DIM, 128), BF),
    ("a_all", (GTOK, DIM), BF),
    ("pre", (GTOK, 256), F32),
    ("cos", (GTOK, 128), F32),
    ("sin", (GTOK, 128), F32),
    ("qr", (GTOK, 128), BF),
    ("kr", (GTOK, 128), BF),
    ("vv", (GTOK, 128), BF),
    ("mixed", (GTOK, 128), F32),
    ("level", (GTOK, 128), F32),
    ("o_rows", (8, ROWS, 128), BF),
    ("o_to", (8, ROWS, 128), BF),
    ("w_out", (DIM, DIM), BF),
    ("ob", (ROWS, DIM), BF),
    ("x1", (ROWS, DIM), F32),
    ("a2", (ROWS, DIM), BF),
    ("gate", (EXPERTS, ROWS), F32),
    ("gates", (EXPERTS, 8, 128), F32),
    ("gates_to", (EXPERTS, 8, 128), F32),
    ("a2_to", ROW_SLOTS, BF),
    ("a_rows", (EXPERTS * CAP, DIM), BF),
    ("hid", (EXPERTS * CAP, FF), BF),
    ("dy", (EXPERTS * CAP, DIM), BF),
    ("dgu", (EXPERTS * CAP, 2 * FF), BF),
    ("dg_rows", (EXPERTS, 8, ROWS), F32),
    ("dg_to", (EXPERTS, 8, ROWS), F32),
    ("grad", (2, 4, 4, 32, WIDE), BF),
    ("grad_mid", (8, 32, WIDE), BF),
    ("stage", (8, CAP, DIM), BF),
    ("sum", (ROWS, DIM), F32),
    ("dl", (128, ROWS), BF),
    ("dx1", (ROWS, DIM), F32),
    ("db", (ROWS, DIM), BF),
    ("do_rows", (8, ROWS, 128), BF),
    ("do_to", (8, ROWS, 128), BF),
    ("gwo_mid", (16, 4, 8, DIM), BF),
    ("gwo_sum", (16, 8, DIM), BF),
    ("dq", (GTOK, 128), F32),
    ("dk", (GTOK, 128), F32),
    ("dv", (GTOK, 128), F32),
    ("dqkv", (GTOK, 256), BF),
    ("dq_to", (8, ROWS, 256), BF),
    ("dq_all", (ROWS, 2 * DIM), BF),
    ("wall_rows", (2, 16, 8, 2 * DIM), BF),
    ("gain_one_grad", (1, DIM), F32),
    ("gain_q_grad", (1, 128), F32),
    ("gain_k_grad", (1, 128), F32),
    ("hg_co", (8, 2, 4, 8, 384), BF),
    ("hg_mid", (8, 2, 4, 8, 384), BF),
    ("hg_z", (4, 8, 2, 8, 384), BF),
    ("hg_sum", (8, 2, 8, 384), BF),
)
SEMS = dict(s_stage=1, s_fetch=2, s_x=11)
PAIR_SEMS = ("s_dz", "s_a2", "s_gate", "s_da", "s_dg", "s_y")
SEMS.update(dict.fromkeys(PAIR_SEMS, 8))
SEND_SEMS = """s_picks s_heads s_heads_pass s_heads_co s_gu s_dn s_wide s_out s_out_z s_out_co s_all s_all_x s_all_co
s_o s_grad s_grad_last s_do s_dq s_gwo_co s_gwo_x s_gwo s_hg_co s_hg_z s_hg"""
SEMS.update(dict.fromkeys(SEND_SEMS.split(), 2))


def layer(*operands):
    names = [name for name, *_ in INPUTS + OUTPUTS + LANDING + SCRATCH] + list(SEMS)

    def body(*refs):
        layer_kernel(types.SimpleNamespace(**dict(zip(names, refs))))

    return pl.pallas_call(
        body,
        out_shape=[jax.ShapeDtypeStruct(shape, kind) for _, shape, kind in OUTPUTS + LANDING],
        in_specs=[pl.BlockSpec(memory_space=space) for _, space in INPUTS],
        out_specs=[pl.BlockSpec(memory_space=pltpu.VMEM)] * len(OUTPUTS)
        + [pl.BlockSpec(memory_space=pl.ANY)] * len(LANDING),
        scratch_shapes=[pltpu.VMEM(shape, kind) for _, shape, kind in SCRATCH]
        + [pltpu.SemaphoreType.DMA((n,)) for n in SEMS.values()],
        compiler_params=pltpu.CompilerParams(
            collective_id=0, has_side_effects=True, vmem_limit_bytes=VMEM_LIMIT
        ),
        name="layer",
    )(*operands)


VMEM_LIMIT = 63 << 20


def finish_kernel(
    output, grad_inputs, hg, gwo, experts, o_output, o_inputs, o_q, o_k, o_v, o_out, o_router, o_gains, o_gu, o_dn
):
    o_output[...] = output[...]
    o_inputs[...] = grad_inputs[...]
    heads = [hg[2 * c].astype(F32) + hg[2 * c + 1].astype(F32) for c in range(8)]
    for c in range(8):
        o_q[:, c * 128 : (c + 1) * 128] = heads[c][:, :128]
    for c in range(4):
        at, two = slice(c * 128, (c + 1) * 128), heads[2 * c : 2 * c + 2]
        o_k[:, at] = jnp.concatenate([head[:, 128:192] for head in two], axis=1)
        o_v[:, at] = jnp.concatenate([head[:, 192:256] for head in two], axis=1)
    side = sum(head[:, 256:] for head in heads)
    o_router[...] = side[:, :EXPERTS]
    o_gains[...] = side[:1, EXPERTS : EXPERTS + GAINS]
    o_out[...] = sum(gwo[n].astype(F32) for n in range(16))
    o_gu[...] = experts[:, :, : 2 * FF].astype(F32)
    o_dn[...] = experts[:, :, 2 * FF :].astype(F32)


def finish(*operands):
    shapes = (
        ((ROWS, DIM), BF),
        ((ROWS, DIM), BF),
        ((8, HEADS * HEAD), F32),
        ((8, KV_HEADS * HEAD), F32),
        ((8, KV_HEADS * HEAD), F32),
        ((8, DIM), F32),
        ((8, EXPERTS), F32),
        ((1, GAINS), F32),
        ((8, 32, 2 * FF), F32),
        ((8, 32, FF), F32),
    )
    vmem = pl.BlockSpec(memory_space=pltpu.VMEM)
    return pl.pallas_call(
        finish_kernel,
        out_shape=[jax.ShapeDtypeStruct(shape, kind) for shape, kind in shapes],
        in_specs=[vmem] * len(operands),
        out_specs=[vmem] * len(shapes),
        compiler_params=pltpu.CompilerParams(vmem_limit_bytes=VMEM_LIMIT),
        name="finish",
    )(*operands)


def shards(
    inputs,
    cotangent,
    w_query,
    key_weight,
    value_weight,
    w_output,
    w_router,
    norm_gains,
    w_gate_up,
    w_down,
    seq_lengths,
    block_map,
    routes,
    priority,
):
    output, grad_inputs, hg, gwo, experts, *_ = layer(
        seq_lengths[0],
        block_map[0],
        inputs[0],
        cotangent[0],
        w_query,
        key_weight,
        value_weight,
        w_router,
        norm_gains[None],
        w_output.T,
        routes[0].T,
        priority[0],
        w_gate_up,
        jnp.swapaxes(w_down, 1, 2),
    )
    output, grad_inputs, q, k, v, out, router, gains, gate_up, down = finish(
        output, grad_inputs, hg, gwo, experts
    )
    return (
        output[None],
        grad_inputs[None],
        q,
        k,
        v,
        out.T,
        router,
        gains[0],
        gate_up,
        jnp.swapaxes(down, 1, 2),
    )


def solution(mesh):
    groups = ("yh", "co", "z")
    specs = (
        P(groups, CTX, None),
        P(groups, CTX, None),
        P(ALL, None),
        P(ALL, None),
        P(ALL, None),
        P(None, ALL),
        P(ALL, None),
        P(ALL),
        P(("yh", "co"), WT, None),
        P(("yh", "co"), None, WT),
        P(groups, None),
        P(groups, None),
        P(groups, CTX, None),
        P(groups, CTX, None),
    )
    return jax.shard_map(
        shards,
        mesh=Mesh(mesh.devices.reshape(SIZES), ALL),
        in_specs=specs,
        out_specs=specs[:10],
        check_vma=False,
    )
```

time: 276 us -> 234 us (0.85)
  Pallas kernels: 255 us -> 229 us
  local copies, waits for them, and re-layouts: 14.3 us -> 0 us
  other arithmetic: 4.59 us -> 0 us
    pallas_call x1, Pallas kernels: 255 us -> 226 us  [layer(): pl.pallas_call(body, out_shape=[jax.ShapeDtypeStruct(shape, kind) for _,...]
    reshape x7 -> x0, local copies, waits for them, and re-layouts: 4.31 us -> none  [the longest x1 1.37 us: shards(): rows[..., :128].reshape(8, HEADS * HEAD)]
    slice x5 -> x0, local copies, waits for them, and re-layouts: 3.64 us -> none  [the longest x1 2.13 us: shards(): expert_grad[..., :2 * FF]]
    concatenate x2 -> x0, other arithmetic: 3.43 us -> none  [the longest x1 2.06 us: shards(): wide = jnp.concatenate([w_gate_up, jnp.swapaxes(w_down, 1, 2)], axis=-1)]
    pallas_call x0 -> x1, Pallas kernels: none -> 2.8 us  [finish(): pl.pallas_call(finish_kernel, out_shape=[jax.ShapeDtypeStruct(shape, kind...]
where the time goes in v1:
time: 234 us; the launch traced here: 230 us
  Pallas kernels  229 us (98%)
    pallas_call x1, Pallas kernels, layer(): pl.pallas_call(body, out_shape=[jax.ShapeDtypeStruct(shape, kind) for _,...  226 us

profile of v1, /device:TPU:1, one launch (start us, length us, event | category | flops | bytes accessed | tf_op | source)
XLA Modules:
  0.0 229.8 jit_solution(15070848177448279368)
XLA Ops:
  0.6 226.3 %layer.1 = (bf16[128,1024]{1,0:T(8,128)(2,1)}, bf16[128,1024]{1,0:T(8,128)(2,1)}, bf16[16,8,384]{2,1,0:T(8,128)(2,1)}, bf16[16,8,1024]{2,1,0:T(8,128)(2,1)}, bf1...) custom-call(s32[4]{0:T(128)} %bitcast.21, ...), custom_call_target="tpu_custom_call" | custom-call | tf_op jit(solution)/shard_map/layer/pallas_call | solution.py:1025
  227.0 2.8 %finish.1 = (bf16[128,1024]{1,0:T(8,128)(2,1)}, bf16[128,1024]{1,0:T(8,128)(2,1)}, f32[8,1024]{1,0:T(8,128)}, f32[8,512]{1,0:T(8,128)}, f32[8,512]{1,0:T(8,128)}...) custom-call(bf16[128,1024]{1,0:T(8,128)(2,1)} %get-tuple-element.25., ...), custom_call_target="tpu_custom_call" | custom-call | tf_op jit(solution)/shard_map/finish/pallas_call | solution.py:1077

commit v2 on v1

--- a/solution.py
+++ b/solution.py
@@ -131,9 +131,9 @@
         self.blocks, self.landing, self.sems, self.me = blocks, landing, sems, linear(EP)
 
     def start(self, c):
-        yh, co = spin("yh", lax.div(c, 2)), spin("co", lax.rem(c, 2))
+        yl, co = spin("yl", lax.div(c, 2)), spin("co", lax.rem(c, 2))
         for j in range(8):
-            yl, z = spin("yl", j // 4), spin("z", j % 4)
+            yh, z = spin("yh", j // 4), spin("z", j % 4)
             place = ((yh * 2 + co) * 2 + yl) * 4 + z
             copy = remote(
                 self.blocks.at[place],
@@ -357,18 +357,18 @@
         own=False,
     )
     send_out = Send(
-        LONG,
+        FLAT,
         lambda p: r.out,
-        lambda q: r.out_to.at[q, core, deep],
-        lambda n: r.out_to.at[pl.ds(0, n), core, deep],
+        lambda q: r.out_to.at[q, core, spot],
+        lambda n: r.out_to.at[pl.ds(0, n), core, spot],
         r.s_out,
     )
     pass_out = Send(
-        ("z",),
-        lambda p: r.out_to.at[:, core, deep],
+        ("x",),
+        lambda p: r.out_to.at[:, core, spot],
         lambda q: r.out_to.at[:, core, q],
         lambda n: r.out_to.at[:, core, pl.ds(0, n)],
-        r.s_out_z,
+        r.s_out_x,
         own=False,
     )
     swap_out = Send(
@@ -486,6 +486,9 @@
     send_dn.start()
 
     send_picks.wait()
+    drain(r.x, r.s_x.at[4])
+    for i in range(1, 4):
+        pass_x.copy(i, 4 + i, 10).start()
     mine = jnp.zeros((16, 128), I32)
     for p in range(8):
         mine = mine + r.picks_to[p] * (r.blocks[p] == place).astype(I32)
@@ -500,25 +503,37 @@
     for e in range(EXPERTS):
         r.hot[pl.ds(e * CAP, CAP)] = (rank[e : e + 1] == seat).astype(F32)
 
-    def part_of(c):
-        return spin("yh", lax.div(c, 2)) * 2 + spin("co", lax.rem(c, 2))
+    def runs(c):
+        four = spin("co", lax.rem(c, 2)) * 8 + spin("yl", lax.div(c, 2)) * 4
+        return four, four + 16
+
+    def take(ref, c):
+        return jnp.concatenate([ref[pl.ds(four, 4)] for four in runs(c)], axis=0)
+
+    def put(ref, c, v):
+        for n, four in enumerate(runs(c)):
+            ref[pl.ds(four, 4)] = v[4 * n : 4 * n + 4]
+
+    def stage(ref, c):
+        for n, four in enumerate(runs(c)):
+            pltpu.make_async_copy(
+                ref.at[pl.ds(four, 4)], r.stage.at[pl.ds(4 * n, 4)], r.s_stage.at[0]
+            ).start()
+
+    def staged():
+        drain(r.stage, r.s_stage.at[0])
+
+    def hot_part(c):
+        return jnp.concatenate(
+            [r.hot[pl.ds(pl.multiple_of(four * CAP, 4 * CAP), 4 * CAP)] for four in runs(c)], axis=0
+        )
 
     def fill(source, rows, c):
-        for i in range(2):
-            eight = part_of(c) * 8 + 4 * i
-            at = pl.ds(pl.multiple_of(eight * CAP, 4 * CAP), 4 * CAP)
-            part = dot(r.hot[at].astype(BF), source[...])
-            rows[pl.ds(eight, 4)] = part.reshape(4, CAP, DIM).astype(BF)
-
-    drain(r.x, r.s_x.at[4])
-    for i in range(1, 4):
-        pass_x.copy(i, 4 + i, 10).start()
+        part = dot(hot_part(c).astype(BF), source[...])
+        put(rows, c, part.reshape(8, CAP, DIM).astype(BF))
+
     send_heads.wait()
     pass_heads.start()
-    send_out.wait()
-    pass_out.start()
-    pass_heads.wait()
-    swap_heads.start()
 
     def fill_dz(c, carry):
         fill(r.dz, r.dz_rows, c)
@@ -526,6 +541,11 @@
         return carry
 
     lax.fori_loop(0, 4, fill_dz, 0)
+    send_all.start()
+    pass_heads.wait()
+    swap_heads.start()
+    send_out.wait()
+    pass_out.start()
     swap_heads.wait()
 
     packed = r.heads_to[...].astype(F32).reshape(128, 8, 384)
@@ -572,10 +592,6 @@
     drain(r.x, r.s_x.at[8])
     for n in (9, 10):
         drain(send_x.slots(3), r.s_x.at[n])
-    send_gu.wait()
-    send_dn.wait()
-    pass_wide.start()
-    send_all.start()
 
     def stacked(v):
         v = v.astype(F32)
@@ -603,12 +619,19 @@
         r.o_rows[tile] = result.astype(BF)
         r.level[at] = beside(jnp.broadcast_to(top + jnp.log(total), (2 * ROWS, 128)))
     send_o.start()
+    send_gu.wait()
+    send_dn.wait()
+    pass_wide.start()
     pass_out.wait()
     swap_out.start()
     swap_out.wait()
 
     def lay(i, carry):
-        r.w_out[rows_of(i)] = merge(r.out_to[pl.ds(2 * i, 2)])
+        rows = [
+            r.out_to[pl.ds((lax.div(i, 4) * 2 + n // 2) * 4, 4), n % 2, lax.rem(i, 4)]
+            for n in range(4)
+        ]
+        r.w_out[rows_of(i)] = merge(jnp.concatenate(rows, axis=0))
         return carry
 
     lax.fori_loop(0, 8, lay, 0)
@@ -628,7 +651,8 @@
     chosen = jnp.where(named, probs, 0.0)
     total = jnp.sum(chosen, axis=0, keepdims=True)
     gate = chosen / total
-    r.gate[...] = gate
+    for n in range(8):
+        r.gate[n] = gate[4 * n : 4 * n + 4]
     r.gates[:, 0, :] = gate
     r.gates[:, 1, :] = rank
     send_gate.start_all()
@@ -650,21 +674,20 @@
     def work(c, carry):
         send_gate.arrived(c)
         send_dz.arrived(c)
-        k8 = part_of(c) * 8
         at = pl.ds(pl.multiple_of(c * PART, PART), PART)
-        staged = bring(r.dz_to.at[pl.ds(k8, 8)], r.stage)
+        stage(r.dz_to, c)
         send_a2.arrived(c)
-        a = merge(r.a2_to[pl.ds(k8, 8)])
+        a = merge(take(r.a2_to, c))
         r.a_rows[at] = a
         gu = dot(a, w_gu[...])
         g, up = gu[:, :FF], gu[:, FF:]
         s = 1.0 / (1.0 + jnp.exp(-g))
         hid = (g * s * up).astype(BF)
         r.hid[at] = hid
-        note = r.gates_to[pl.ds(k8, 8)]
+        note = take(r.gates_to, c)
         kept = note[:, 1:2] == seat[None]
         column = jnp.sum(jnp.where(kept, note[:, 0:1], 0.0), axis=2, keepdims=True)
-        staged.wait()
+        staged()
         dz_part = r.stage[...].astype(F32)
         dy = (dz_part * column).reshape(PART, DIM).astype(BF)
         r.dy[at] = dy
@@ -674,13 +697,13 @@
         r.dgu[at] = dgu
         da = dot(dgu, w_gu[...], ((1,), (1,)))
         send_a2.sent(c)
-        r.a2_rows[pl.ds(k8, 8)] = da.reshape(8, CAP, DIM).astype(BF)
+        put(r.a2_rows, c, da.reshape(8, CAP, DIM).astype(BF))
         send_da.start(c)
         y = dot(hid, w_dn[...], ((1,), (1,))).reshape(8, CAP, DIM).astype(BF)
-        r.dz_rows[pl.ds(k8, 8)] = y
+        put(r.dz_rows, c, y)
         inner = jnp.sum(y.astype(F32) * dz_part, axis=2, keepdims=True)
         inner = jnp.sum(jnp.where(kept, inner, 0.0), axis=1, keepdims=True)
-        r.dg_rows[pl.ds(k8, 8)] = jnp.broadcast_to(inner, (8, 8, ROWS))
+        put(r.dg_rows, c, jnp.broadcast_to(inner, (8, 8, ROWS)))
         send_dg.start(c)
         return carry
 
@@ -715,16 +738,16 @@
     r.dl[...] = dl
     r.sum[...] = dot(dl, r.router[...], ((0,), (1,)))
 
-    def hot_part(c):
-        return r.hot[pl.ds(pl.multiple_of(part_of(c) * PART, PART), PART)]
-
     def unmix(c, carry):
         send_da.arrived(c)
-        bring(r.da_to.at[pl.ds(part_of(c) * 8, 8)], r.stage).wait()
+        stage(r.da_to, c)
+        staged()
         r.sum[...] += dot(hot_part(c).astype(BF), merge(r.stage[...]), ((0,), (0,)))
         return carry
 
     lax.fori_loop(0, 4, unmix, 0)
+    send_y.start(0)
+    send_y.start(1)
     dx_two, terms_two = norm_back(r.x1[...], rms(r.x1[...]), gain_two, r.sum[...])
     gain_two_grad = jnp.sum(terms_two, axis=0, keepdims=True)
     r.dx1[...] = dz + dx_two
@@ -733,9 +756,8 @@
     for h in range(8):
         r.do_rows[h] = do[:, h * 128 : (h + 1) * 128]
     send_do.start()
-
-    send_y.start(0)
-    send_y.start(1)
+    send_y.start(2)
+    send_y.start(3)
 
     def spread_out(i, carry):
         part = dot(r.db[:, rows_of(i)], r.ob[...], ((0,), (0,)))
@@ -776,7 +798,6 @@
     swap_gwo.wait()
     bring(r.gwo_co, r.gwo_mid).wait()
     lax.fori_loop(0, 16, add_core, 0)
-    pass_gwo.start()
     r.gain_q_grad[...] = jnp.zeros_like(r.gain_q_grad)
     r.gain_k_grad[...] = jnp.zeros_like(r.gain_k_grad)
 
@@ -803,6 +824,17 @@
 
     lax.fori_loop(1, 9, back, 0)
     send_dq.start_own()
+    send_grad.wait()
+    bring(r.grad_to, r.wide_to).wait()
+
+    def add_grad(i, carry):
+        total = sum(r.wide_to[lax.div(i, 4), n, lax.rem(i, 4)].astype(F32) for n in range(4))
+        r.grad_mid[i] = total.astype(BF)
+        return carry
+
+    lax.fori_loop(0, 8, add_grad, 0)
+    last_grad.start()
+    pass_gwo.start()
 
     diagonal = lax.broadcasted_iota(I32, (ROWS, 128), 0) == lax.broadcasted_iota(I32, (ROWS, 128), 1)
 
@@ -828,35 +860,9 @@
     ).reshape(DIM, 128) + dot(r.a2[...], r.dl[...], ((0,), (1,)))
     r.heads_to[:, :, :, :, :, pl.ds(256, 128)] = side.reshape(8, 2, 2, 4, 8, 128).astype(BF)
     swap_hg.start()
-
-    send_grad.wait()
-    bring(r.grad_to, r.wide_to).wait()
-
-    def add_grad(i, carry):
-        total = sum(r.wide_to[lax.div(i, 4), n, lax.rem(i, 4)].astype(F32) for n in range(4))
-        r.grad_mid[i] = total.astype(BF)
-        return carry
-
-    lax.fori_loop(0, 8, add_grad, 0)
-    last_grad.start()
     swap_hg.wait()
     r.hg_mid[...] = (r.heads_to[:, :, core].astype(F32) + r.hg_co[...].astype(F32)).astype(BF)
     pass_hg.start()
-    send_y.start(2)
-    send_y.start(3)
-    pass_gwo.wait()
-    bring(r.gwo_x, r.out_to.at[:, 0]).wait()
-
-    def add_spot(i, carry):
-        total = sum(r.out_to[i, 0, n].astype(F32) for n in range(4))
-        r.gwo_sum[i] = total.astype(BF)
-        return carry
-
-    lax.fori_loop(0, 16, add_spot, 0)
-    last_gwo.start()
-    pass_hg.wait()
-    r.hg_sum[...] = sum(r.hg_z[n].astype(F32) for n in range(4)).astype(BF)
-    last_hg.start()
 
     send_dq.wait()
     swap_all.wait()
@@ -888,14 +894,31 @@
     dx_one, _ = norm_back(x_own, rms(x_own), gain_one, r.sum[...])
     r.grad_inputs[...] = (r.dx1[...] + dx_one).astype(BF)
 
+    pass_hg.wait()
+    r.hg_sum[...] = sum(r.hg_z[n].astype(F32) for n in range(4)).astype(BF)
+    last_hg.start()
+    pass_gwo.wait()
+    bring(r.gwo_x, r.out_to.at[:, 0]).wait()
+
+    def add_spot(i, carry):
+        total = sum(r.out_to[i, 0, n].astype(F32) for n in range(4))
+        r.gwo_sum[i] = total.astype(BF)
+        return carry
+
+    lax.fori_loop(0, 16, add_spot, 0)
+    last_gwo.start()
+
     r.sum[...] = r.x1[...]
+
+    def gates_of(c):
+        return jnp.concatenate([r.gate[lax.div(four, 4)] for four in runs(c)], axis=0)
 
     def mix(c, carry):
         send_y.arrived(c)
-        k8 = pl.multiple_of(part_of(c) * 8, 8)
-        bring(r.y_to.at[pl.ds(k8, 8)], r.stage).wait()
+        stage(r.y_to, c)
+        staged()
         y = merge(r.stage[...])
-        weights = hot_part(c).reshape(8, CAP, ROWS) * r.gate[pl.ds(k8, 8)][:, None]
+        weights = hot_part(c).reshape(8, CAP, ROWS) * gates_of(c)[:, None]
         weights = weights.reshape(PART, ROWS)
         high = weights.astype(BF)
         low = (weights - high.astype(F32)).astype(BF)
@@ -972,7 +995,7 @@
     ("ob", (ROWS, DIM), BF),
     ("x1", (ROWS, DIM), F32),
     ("a2", (ROWS, DIM), BF),
-    ("gate", (EXPERTS, ROWS), F32),
+    ("gate", (8, 4, ROWS), F32),
     ("gates", (EXPERTS, 8, 128), F32),
     ("gates_to", (EXPERTS, 8, 128), F32),
     ("a2_to", ROW_SLOTS, BF),
@@ -1011,7 +1034,7 @@
 SEMS = dict(s_stage=1, s_fetch=2, s_x=11)
 PAIR_SEMS = ("s_dz", "s_a2", "s_gate", "s_da", "s_dg", "s_y")
 SEMS.update(dict.fromkeys(PAIR_SEMS, 8))
-SEND_SEMS = """s_picks s_heads s_heads_pass s_heads_co s_gu s_dn s_wide s_out s_out_z s_out_co s_all s_all_x s_all_co
+SEND_SEMS = """s_picks s_heads s_heads_pass s_heads_co s_gu s_dn s_wide s_out s_out_x s_out_co s_all s_all_x s_all_co
 s_o s_grad s_grad_last s_do s_dq s_gwo_co s_gwo_x s_gwo s_hg_co s_hg_z s_hg"""
 SEMS.update(dict.fromkeys(SEND_SEMS.split(), 2))
 

time: 234 us -> 212 us (0.906); the launches traced: 230 us -> 211 us
  Pallas kernels: 229 us -> 210 us
    pallas_call x1, Pallas kernels: 226 us -> 208 us  [layer(): pl.pallas_call(body, out_shape=[jax.ShapeDtypeStruct(shape, kind) for _,...]
where the time goes in v2:
time: 212 us; the launch traced here: 211 us
  Pallas kernels  210 us (99%)
    pallas_call x1, Pallas kernels, layer(): pl.pallas_call(body, out_shape=[jax.ShapeDtypeStruct(shape, kind) for _,...  208 us

profile of v2, /device:TPU:1, one launch (start us, length us, event | category | flops | bytes accessed | tf_op | source)
XLA Modules:
  0.0 211.0 jit_solution(16578866333881729568)
XLA Ops:
  0.6 207.5 %layer.1 = (bf16[128,1024]{1,0:T(8,128)(2,1)}, bf16[128,1024]{1,0:T(8,128)(2,1)}, bf16[16,8,384]{2,1,0:T(8,128)(2,1)}, bf16[16,8,1024]{2,1,0:T(8,128)(2,1)}, bf1...) custom-call(s32[4]{0:T(128)} %bitcast.21, ...), custom_call_target="tpu_custom_call" | custom-call | tf_op jit(solution)/shard_map/layer/pallas_call | solution.py:1048
  208.2 2.8 %finish.1 = (bf16[128,1024]{1,0:T(8,128)(2,1)}, bf16[128,1024]{1,0:T(8,128)(2,1)}, f32[8,1024]{1,0:T(8,128)}, f32[8,512]{1,0:T(8,128)}, f32[8,512]{1,0:T(8,128)}...) custom-call(bf16[128,1024]{1,0:T(8,128)(2,1)} %get-tuple-element.25., ...), custom_call_target="tpu_custom_call" | custom-call | tf_op jit(solution)/shard_map/finish/pallas_call | solution.py:1100

commit v3 on v2

--- a/solution.py
+++ b/solution.py
@@ -1034,9 +1034,33 @@
 SEMS = dict(s_stage=1, s_fetch=2, s_x=11)
 PAIR_SEMS = ("s_dz", "s_a2", "s_gate", "s_da", "s_dg", "s_y")
 SEMS.update(dict.fromkeys(PAIR_SEMS, 8))
-SEND_SEMS = """s_picks s_heads s_heads_pass s_heads_co s_gu s_dn s_wide s_out s_out_x s_out_co s_all s_all_x s_all_co
-s_o s_grad s_grad_last s_do s_dq s_gwo_co s_gwo_x s_gwo s_hg_co s_hg_z s_hg"""
-SEMS.update(dict.fromkeys(SEND_SEMS.split(), 2))
+SEND_SEMS = (
+    "s_picks",
+    "s_heads",
+    "s_heads_pass",
+    "s_heads_co",
+    "s_gu",
+    "s_dn",
+    "s_wide",
+    "s_out",
+    "s_out_x",
+    "s_out_co",
+    "s_all",
+    "s_all_x",
+    "s_all_co",
+    "s_o",
+    "s_grad",
+    "s_grad_last",
+    "s_do",
+    "s_dq",
+    "s_gwo_co",
+    "s_gwo_x",
+    "s_gwo",
+    "s_hg_co",
+    "s_hg_z",
+    "s_hg",
+)
+SEMS.update(dict.fromkeys(SEND_SEMS, 2))
 
 
 def layer(*operands):

time: 212 us -> 212 us (level)
  no operation moved by 1% of the time
where the time goes in v3:
time: 212 us; the launch traced here: 211 us
  Pallas kernels  210 us (99%)
    pallas_call x1, Pallas kernels, layer(): pl.pallas_call(body, out_shape=[jax.ShapeDtypeStruct(shape, kind) for _,...  208 us

profile of v3, /device:TPU:1, one launch (start us, length us, event | category | flops | bytes accessed | tf_op | source)
XLA Modules:
  0.0 211.0 jit_solution(16578866333881729568)
XLA Ops:
  0.6 207.5 %layer.1 = (bf16[128,1024]{1,0:T(8,128)(2,1)}, bf16[128,1024]{1,0:T(8,128)(2,1)}, bf16[16,8,384]{2,1,0:T(8,128)(2,1)}, bf16[16,8,1024]{2,1,0:T(8,128)(2,1)}, bf1...) custom-call(s32[4]{0:T(128)} %bitcast.21, ...), custom_call_target="tpu_custom_call" | custom-call | tf_op jit(solution)/shard_map/layer/pallas_call | solution.py:1072
  208.2 2.8 %finish.1 = (bf16[128,1024]{1,0:T(8,128)(2,1)}, bf16[128,1024]{1,0:T(8,128)(2,1)}, f32[8,1024]{1,0:T(8,128)}, f32[8,512]{1,0:T(8,128)}, f32[8,512]{1,0:T(8,128)}...) custom-call(bf16[128,1024]{1,0:T(8,128)(2,1)} %get-tuple-element.25., ...), custom_call_target="tpu_custom_call" | custom-call | tf_op jit(solution)/shard_map/finish/pallas_call | solution.py:1124

commit v4 on v3

--- a/solution.py
+++ b/solution.py
@@ -537,7 +537,11 @@
 
     def fill_dz(c, carry):
         fill(r.dz, r.dz_rows, c)
-        send_dz.start(c)
+
+        @pl.when(c < 3)
+        def _():
+            send_dz.start(c)
+
         return carry
 
     lax.fori_loop(0, 4, fill_dz, 0)
@@ -660,6 +664,11 @@
     def fill_a2(c, carry):
         fill(r.a2, r.a2_rows, c)
         send_a2.start(c)
+
+        @pl.when(c == 2)
+        def _():
+            send_dz.start(3)
+
         return carry
 
     lax.fori_loop(0, 4, fill_a2, 0)

time: 212 us -> 211 us (level)
  no operation moved by 1% of the time
where the time goes in v4:
time: 211 us; the launch traced here: 210 us
  Pallas kernels  209 us (99%)
    pallas_call x1, Pallas kernels, layer(): pl.pallas_call(body, out_shape=[jax.ShapeDtypeStruct(shape, kind) for _,...  206 us

profile of v4, /device:TPU:1, one launch (start us, length us, event | category | flops | bytes accessed | tf_op | source)
XLA Modules:
  0.0 209.9 jit_solution(4440395803089907956)
XLA Ops:
  0.6 206.5 %layer.1 = (bf16[128,1024]{1,0:T(8,128)(2,1)}, bf16[128,1024]{1,0:T(8,128)(2,1)}, bf16[16,8,384]{2,1,0:T(8,128)(2,1)}, bf16[16,8,1024]{2,1,0:T(8,128)(2,1)}, bf1...) custom-call(s32[4]{0:T(128)} %bitcast.21, ...), custom_call_target="tpu_custom_call" | custom-call | tf_op jit(solution)/shard_map/layer/pallas_call | solution.py:1081
  207.1 2.8 %finish.1 = (bf16[128,1024]{1,0:T(8,128)(2,1)}, bf16[128,1024]{1,0:T(8,128)(2,1)}, f32[8,1024]{1,0:T(8,128)}, f32[8,512]{1,0:T(8,128)}, f32[8,512]{1,0:T(8,128)}...) custom-call(bf16[128,1024]{1,0:T(8,128)(2,1)} %get-tuple-element.25., ...), custom_call_target="tpu_custom_call" | custom-call | tf_op jit(solution)/shard_map/finish/pallas_call | solution.py:1133
